TPU v7x, 256 devices: a whole 4x4x8 slice. The times are simulated.
256 devices in a mesh: dp: 16 (over y_hi, z), mp: 16 (over x, y_lo, core).
Axes of the slice: x: 4, y: 4 (y_hi: 2, y_lo: 2; y = y_hi * 2 + y_lo), z: 8, core: 2. Of those that a mesh axis runs over, the one named last changes fastest.
Arguments:
- normed: bfloat16 [6144, 9216], P(('dp', 'mp')), may hold values from -6 to 6
- w_query: bfloat16 [9216, 8192], P(None, 'mp'), may hold values from -0.0625 to 0.0625
- w_key: bfloat16 [9216, 256], P(None, 'mp'), may hold values from -0.0625 to 0.0625
- w_value: bfloat16 [9216, 256], P(None, 'mp'), may hold values from -0.0625 to 0.0625
- query: bfloat16 [6144, 8192], P('dp', 'mp'), may hold values from -42 to 42
- key: bfloat16 [6144, 256], P('dp'), may hold values from -6 to 6
- value: bfloat16 [6144, 256], P('dp'), may hold values from -6 to 6
- grad_context: bfloat16 [6144, 8192], P('dp', 'mp'), may hold values from -12 to 12
Outputs:
- grad_input: bfloat16 [6144, 9216], P(('dp', 'mp'))
- grad_wq: bfloat16 [9216, 8192], P('dp', 'mp')
- grad_wk: bfloat16 [9216, 256], P('dp', 'mp')
- grad_wv: bfloat16 [9216, 256], P('dp', 'mp')
All inputs are finite; a program needn't handle non-finite values.
Results may differ from a plain program's by a relative error of at most 0.04.
Values may be sent and summed in bfloat16 or wider, within the bound.
A program may use at most 128 MiB of HBM per device.

v0:
```python
import jax
import jax.numpy as jnp
from jax import lax
from jax.sharding import PartitionSpec as P

HEAD_DIM = 256


def shards(normed, w_query, w_key, w_value, query, key, value, grad_context):
    gathered = lax.all_gather(normed, "mp", axis=0, tiled=True)
    rows = query.shape[0]
    heads_local = query.shape[1] // HEAD_DIM
    scale = HEAD_DIM ** (-0.5)
    q_heads = query.reshape(rows, heads_local, HEAD_DIM)
    g_heads = grad_context.reshape(rows, heads_local, HEAD_DIM)
    scores = jnp.einsum("thd,sd->hts", q_heads, key, preferred_element_type=jnp.float32) * scale
    causal = lax.broadcasted_iota(jnp.int32, (rows, rows), 0) >= lax.broadcasted_iota(
        jnp.int32, (rows, rows), 1
    )
    scores = jnp.where(causal[None], scores, -jnp.inf)
    top = jnp.max(scores, axis=-1, keepdims=True)
    expo = jnp.exp(scores - top)
    probs = expo / jnp.sum(expo, axis=-1, keepdims=True)
    probs_low = probs.astype(jnp.bfloat16)
    context = jnp.einsum("hts,sd->thd", probs_low, value, preferred_element_type=jnp.float32)
    delta = jnp.sum(g_heads.astype(jnp.float32) * context, axis=-1)
    dprob = jnp.einsum("thd,sd->hts", g_heads, value, preferred_element_type=jnp.float32)
    dscore = (probs * (dprob - jnp.transpose(delta)[:, :, None])).astype(jnp.bfloat16)
    grad_q = (
        (jnp.einsum("hts,sd->thd", dscore, key, preferred_element_type=jnp.float32) * scale)
        .reshape(rows, -1)
        .astype(jnp.bfloat16)
    )
    key_part = (
        jnp.einsum("hts,thd->sd", dscore, q_heads, preferred_element_type=jnp.float32) * scale
    )
    value_part = jnp.einsum("hts,thd->sd", probs_low, g_heads, preferred_element_type=jnp.float32)
    columns = w_key.shape[1]
    grad_k, grad_v = (
        lax.psum_scatter(
            key_part.astype(jnp.bfloat16), "mp", scatter_dimension=1, tiled=True
        ).astype(jnp.float32),
        lax.psum_scatter(
            value_part.astype(jnp.bfloat16), "mp", scatter_dimension=1, tiled=True
        ).astype(jnp.float32),
    )
    grad_k = grad_k.astype(jnp.bfloat16)
    grad_v = grad_v.astype(jnp.bfloat16)
    local_grads = jnp.concatenate([grad_q, grad_k, grad_v], axis=1)
    weight_sum = lax.psum_scatter(
        lax.dot_general(
            gathered, local_grads, (((0,), (0,)), ((), ())), preferred_element_type=jnp.float32
        ).astype(jnp.bfloat16),
        "dp",
        scatter_dimension=0,
        tiled=True,
    )
    query_cols = grad_q.shape[1]
    grad_wq = weight_sum[:, :query_cols]
    grad_wk = weight_sum[:, query_cols : query_cols + columns]
    grad_wv = weight_sum[:, query_cols + columns :]
    contract = (((1,), (1,)), ((), ()))
    total = lax.dot_general(grad_q, w_query, contract, preferred_element_type=jnp.float32)
    total = total + lax.dot_general(grad_k, w_key, contract, preferred_element_type=jnp.float32)
    feature_sums = lax.psum_scatter(
        (
            total + lax.dot_general(grad_v, w_value, contract, preferred_element_type=jnp.float32)
        ).astype(jnp.bfloat16),
        "mp",
        scatter_dimension=1,
        tiled=True,
    )
    grad_input = lax.all_to_all(feature_sums, "mp", split_axis=0, concat_axis=1, tiled=True)
    return (grad_input, grad_wq, grad_wk, grad_wv)


def solution(mesh):
    placed = (
        P(("dp", "mp"), None),
        P(None, "mp"),
        P(None, "mp"),
        P(None, "mp"),
        P("dp", "mp"),
        P("dp", None),
        P("dp", None),
        P("dp", "mp"),
    )
    return jax.shard_map(
        shards,
        mesh=mesh,
        in_specs=placed,
        out_specs=(P(("dp", "mp"), None), P("dp", "mp"), P("dp", "mp"), P("dp", "mp")),
        check_vma=False,
    )
```

profile of v0, /device:TPU:1, one launch (start us, length us, event | category | flops | bytes accessed | tf_op | source)
XLA Modules:
  0.0 539.2 jit_solution(17977042192768480220)
XLA Ops:
  7.2 0.0 copy-start
  7.2 0.0 copy-start.3
  7.2 0.0 copy-start.5
  7.2 0.0 reduce-scatter.7.cloned.1.call-start
  7.3 1.3 copy.76
  8.6 0.0 copy-done.3
  8.6 0.2 copy.50
  8.8 0.0 copy-done.5
  8.8 0.0 copy-start.8
  8.8 0.6 fusion.36
  9.4 0.3 copy-done.8
  9.8 0.4 fusion.11
  10.2 0.3 fusion.8
  10.5 1.1 fusion.13
  11.6 0.0 reduce-scatter.7.cloned.1.call-update
  11.6 0.0 reduce-scatter.9.cloned.1.call-start
  11.7 1.1 fusion.14
  12.8 0.0 reduce-scatter.9.cloned.1.call-update
  12.8 0.0 all-gather.2.cloned.1.call-start
  12.8 0.7 all-gather.2.cloned.1.call-update
  13.5 0.0 reduce-scatter.11.cloned.1.call-start
  13.6 0.4 fusion.10
  14.0 10.5 %fusion.40 = f32[384,9216]{0,1:T(8,128)} fusion(bf16[9216,512]{1,0:T(8,128)(2,1)} %param.9, bf16[384,512]{0,1:T(8,128)(2,1)S(1)} %bitcast.78), kind=kOutput, calls=%fused_computation.42 | convolution fusion | flops 3623878656 | bytes 23986176 | tf_op jit(solution)/shard_map/dot_general | solution.py:63
  24.5 50.4 %reduce-scatter.7.cloned.1.call-done = bf16[384,16]{0,1:T(8,128)(2,1)} async-done(((bf16[384,256]{0,1:T(8,128)(2,1)}), bf16[384,16]{0,1:T(8,128)(2,1)}) %reduce-scatter.7.cloned.1.call-update) | async-done | bytes 12304 | tf_op jit(solution)/shard_map/reduce_scatter | solution.py:40
  74.9 0.0 copy-done
  74.9 7.0 %fusion.39 = f32[384,9216]{0,1:T(8,128)} fusion(bf16[384,16]{0,1:T(8,128)(2,1)} %reduce-scatter.7.cloned.1.call-done, bf16[9216,16]{0,1:T(8,128)(2,1)S(1)} %copy-done), kind=kOutput, calls=%fused_computation.41 | convolution fusion | flops 113246208 | bytes 14462976 | tf_op jit(solution)/shard_map/dot_general | solution.py:64
  81.9 57.4 %reduce-scatter.9.cloned.1.call-done = bf16[384,16]{0,1:T(8,128)(2,1)} async-done(((bf16[384,256]{0,1:T(8,128)(2,1)}), bf16[384,16]{0,1:T(8,128)(2,1)}) %reduce-scatter.9.cloned.1.call-update) | async-done | bytes 12304 | tf_op jit(solution)/shard_map/reduce_scatter | solution.py:43
  139.3 0.0 copy-done.4
  139.3 13.2 %add_convert_fusion = bf16[384,9216]{0,1:T(8,128)(2,1)} fusion(f32[384,9216]{0,1:T(8,128)} %fusion.40, f32[384,9216]{0,1:T(8,128)} %fusion.39, bf16[384,16]{0,1:T(8,128)(2,1)} %reduce-scatter.9.cloned.1.call-done, bf16[9216,16]{0,1:T(8,128)(2,1)S(1)} %copy-done.4), kind=kOutput, calls=%fused_computation.1 | convolution fusion | flops 123863040 | bytes 35696640 | tf_op jit(solution)/shard_map/dot_general | solution.py:67
  152.5 0.0 reduce-scatter.11.cloned.1.call-update
  152.6 0.0 reduce-scatter.13.cloned.1.call-start
  152.6 39.2 %all-gather.2.cloned.1.call-done = bf16[384,9216]{1,0:T(8,128)(2,1)} async-done(((bf16[24,9216]{1,0:T(8,128)(2,1)}), bf16[384,9216]{1,0:T(8,128)(2,1)}) %all-gather.2.cloned.1.call-update) | async-done | bytes 7077904 | tf_op jit(solution)/shard_map/all_gather | solution.py:10
  191.8 0.0 copy-done.6
  191.8 0.0 copy-done.7
  191.8 11.2 %fusion.1 = bf16[9216,544]{0,1:T(8,128)(2,1)} fusion(bf16[384,9216]{1,0:T(8,128)(2,1)} %all-gather.2.cloned.1.call-done, bf16[384,16]{0,1:T(8,128)(2,1)S(1)} %copy-done.6, bf16[384,16]{0,1:T(8,128)(2,1)S(1)} %copy-done.7, bf16[384,512]{0,1:T(8,128)(2,1)S(1)} %bitcast.79), kind=kOutput, calls=%fused_computation.3 | convolution fusion | flops 3856637952 | bytes 17522688 | tf_op jit(solution)/shard_map/dot_general | solution.py:51
  203.1 14.5 %copy.71 = bf16[9216,544]{1,0:T(8,128)(2,1)} copy(bf16[9216,544]{0,1:T(8,128)(2,1)} %fusion.1) | data formatting | bytes 20054016
  217.5 0.0 reduce-scatter.13.cloned.1.call-update
  217.5 63.2 %reduce-scatter.11.cloned.1.call-done = bf16[384,576]{0,1:T(8,128)(2,1)} async-done(((bf16[384,9216]{0,1:T(8,128)(2,1)}), bf16[384,576]{0,1:T(8,128)(2,1)}) %reduce-scatter.11.cloned.1.call-update) | async-done | bytes 442384 | tf_op jit(solution)/shard_map/reduce_scatter | solution.py:65
  280.8 1.3 copy.59
  282.0 15.8 %all_to_all.19 = bf16[16,24,576]{2,1,0:T(8,128)(2,1)S(1)} all-to-all(bf16[16,24,576]{2,1,0:T(8,128)(2,1)S(1)} %bitcast.76), channel_id=1, replica_groups=mesh['dp'=16,'mp'=16] {'mp'}, dimensions={0} | all-to-all | bytes 884736 | tf_op jit(solution)/shard_map/all_to_all | solution.py:73
  297.9 0.1 copy.60
  297.9 0.0 copy-start.1
  297.9 1.2 all_to_all.17
  299.1 230.1 %reduce-scatter.13.cloned.1.call-done = bf16[576,544]{1,0:T(8,128)(2,1)} async-done(((bf16[9216,544]{1,0:T(8,128)(2,1)}), bf16[576,544]{1,0:T(8,128)(2,1)}) %reduce-scatter.13.cloned.1.call-update) | async-done | bytes 626704
  529.2 1.2 fusion.35
  530.3 0.7 copy.74
  531.1 0.7 copy.75
  531.8 0.9 slice.12
  (7 shorter events, 0.1 us)
Async XLA Ops:
  7.2 67.7 %copy-start = (bf16[9216,16]{0,1:T(8,128)(2,1)S(1)}, bf16[9216,16]{0,1:T(8,128)(2,1)}, u32[]{:S(2)}) copy-start(bf16[9216,16]{0,1:T(8,128)(2,1)} %param.10) | copy-start | bytes 884740
  7.2 1.4 copy-start.3
  7.2 1.6 copy-start.5
  7.2 67.7 %reduce-scatter.7.cloned.1.call-start = ((), (), s32[]{:S(2)}) async-start(), calls=%async_computation.5 | async-start | bytes 208896 | tf_op jit(solution)/shard_map/reduce_scatter | solution.py:40
  8.8 0.9 copy-start.8
  11.6 127.7 %reduce-scatter.9.cloned.1.call-start = ((), (), s32[]{:S(2)}) async-start(), calls=%async_computation.6 | async-start | bytes 208896 | tf_op jit(solution)/shard_map/reduce_scatter | solution.py:43
  12.8 179.1 %all-gather.2.cloned.1.call-start = ((), (), s32[]{:S(2)}) async-start(), calls=%async_computation.8 | async-start | bytes 7520256 | tf_op jit(solution)/shard_map/all_gather | solution.py:10
  13.5 267.2 %reduce-scatter.11.cloned.1.call-start = ((), (), s32[]{:S(2)}) async-start(), calls=%async_computation.7 | async-start | bytes 7520256 | tf_op jit(solution)/shard_map/reduce_scatter | solution.py:65
  24.5 114.8 %copy-start.4 = (bf16[9216,16]{0,1:T(8,128)(2,1)S(1)}, bf16[9216,16]{0,1:T(8,128)(2,1)}, u32[]{:S(2)}) copy-start(bf16[9216,16]{0,1:T(8,128)(2,1)} %param.11) | copy-start | bytes 884740
  152.5 39.3 %copy-start.6 = (bf16[384,16]{0,1:T(8,128)(2,1)S(1)}, bf16[384,16]{0,1:T(8,128)(2,1)}, u32[]{:S(2)}) copy-start(bf16[384,16]{0,1:T(8,128)(2,1)} %reduce-scatter.9.cloned.1.call-done) | copy-start | bytes 36868
  152.5 39.3 %copy-start.7 = (bf16[384,16]{0,1:T(8,128)(2,1)S(1)}, bf16[384,16]{0,1:T(8,128)(2,1)}, u32[]{:S(2)}) copy-start(bf16[384,16]{0,1:T(8,128)(2,1)} %reduce-scatter.7.cloned.1.call-done) | copy-start | bytes 36868
  152.6 376.6 %reduce-scatter.13.cloned.1.call-start = ((), (), s32[]{:S(2)}) async-start(), calls=%async_computation.9 | async-start | bytes 12533760
  297.9 234.7 %copy-start.1 = (bf16[9216,16]{0,1:T(8,128)(2,1)S(1)}, bf16[9216,16]{0,1:T(8,128)(2,1)}, u32[]{:S(2)}) copy-start(bf16[9216,16]{0,1:T(8,128)(2,1)} %param.10) | copy-start | bytes 884740
  529.2 2.6 copy-start.2
Sparse Core Ops, SparseCore 0:
  11.7 63.1 reduce-scatter.6
  78.1 61.1 reduce-scatter.8
  141.2 50.6 all-gather.1
  194.3 86.4 reduce-scatter.10
  285.4 243.6 reduce-scatter.12
where the time goes:
time: 542 us; the launch traced here: 539 us
  waiting for transfers between devices  441 us (81%)
  matrix products  45.8 us (8%)
  local copies, waits for them, and re-layouts  22.3 us (4%)
  blocking collectives  15.8 us (3%)
  between operations  13.9 us (3%)
    unnamed x6, waiting for transfers between devices  231 us
    reduce_scatter x1, waiting for transfers between devices, shards(): lax.psum_scatter((total + lax.dot_general(grad_v, w_value, contract, pref...  63.2 us
    reduce_scatter x1, waiting for transfers between devices, shards(): lax.psum_scatter(value_part.astype(jnp.bfloat16), 'mp', scatter_dimension...  57.4 us
    reduce_scatter x1, waiting for transfers between devices, shards(): lax.psum_scatter(key_part.astype(jnp.bfloat16), 'mp', scatter_dimension=1...  50.4 us
    all_gather x1, waiting for transfers between devices, shards(): gathered = lax.all_gather(normed, 'mp', axis=0, tiled=True)  39.2 us
    unnamed x22, local copies, waits for them, and re-layouts  16.5 us
    all_to_all x1, blocking collectives, shards(): lax.all_to_all(feature_sums, 'mp', split_axis=0, concat_axis=1, tiled=True)  15.8 us
    dot_general x1, matrix products, shards(): lax.dot_general(grad_v, w_value, contract, preferred_element_type=jnp.flo...  13.2 us
  transfers between devices with their start and end apart: 5, of which 5 were waited for; matrix products, arithmetic and copies ran while one was open for 11% of the time, Pallas kernels for 0%

commit v1 on v0

v1 whole, which is shorter than its diff:
```python
import jax
import jax.numpy as jnp
from jax import lax
from jax.sharding import PartitionSpec as P

HEAD_DIM = 256
Z_GROUPS = [list(range(0, 8)), list(range(8, 16))]
Y_GROUPS = [[z, z + 8] for z in range(8)]


def shards(normed, w_query, w_key, w_value, query, key, value, grad_context):
    rows = query.shape[0]
    heads_local = query.shape[1] // HEAD_DIM
    scale = HEAD_DIM ** (-0.5)
    exchanged = lax.all_to_all(
        jnp.transpose(normed.reshape(normed.shape[0], 2, 8, -1), (2, 0, 1, 3)).reshape(
            8, normed.shape[0], -1
        ),
        "dp", split_axis=0, concat_axis=0, axis_index_groups=Z_GROUPS, tiled=True,
    )
    gathered = lax.all_gather(exchanged, "mp", axis=0, tiled=False)
    gathered = jnp.transpose(gathered, (1, 0, 2, 3)).reshape(8 * rows, -1)
    q_heads = query.reshape(rows, heads_local, HEAD_DIM)
    g_heads = grad_context.reshape(rows, heads_local, HEAD_DIM)
    scores = jnp.einsum("thd,sd->hts", q_heads, key, preferred_element_type=jnp.float32) * scale
    causal = lax.broadcasted_iota(jnp.int32, (rows, rows), 0) >= lax.broadcasted_iota(
        jnp.int32, (rows, rows), 1
    )
    scores = jnp.where(causal[None], scores, -jnp.inf)
    top = jnp.max(scores, axis=-1, keepdims=True)
    expo = jnp.exp(scores - top)
    probs = expo / jnp.sum(expo, axis=-1, keepdims=True)
    probs_low = probs.astype(jnp.bfloat16)
    context = jnp.einsum("hts,sd->thd", probs_low, value, preferred_element_type=jnp.float32)
    delta = jnp.sum(g_heads.astype(jnp.float32) * context, axis=-1)
    dprob = jnp.einsum("thd,sd->hts", g_heads, value, preferred_element_type=jnp.float32)
    dscore = (probs * (dprob - jnp.transpose(delta)[:, :, None])).astype(jnp.bfloat16)
    grad_q = (
        (jnp.einsum("hts,sd->thd", dscore, key, preferred_element_type=jnp.float32) * scale)
        .reshape(rows, -1)
        .astype(jnp.bfloat16)
    )
    key_part = (
        jnp.einsum("hts,thd->ds", dscore, q_heads, preferred_element_type=jnp.float32) * scale
    )
    value_part = jnp.einsum("hts,thd->ds", probs_low, g_heads, preferred_element_type=jnp.float32)
    columns = w_key.shape[1]
    kv = jnp.concatenate(
        [key_part.reshape(-1, columns, rows), value_part.reshape(-1, columns, rows)], axis=1
    ).astype(jnp.bfloat16)
    kv = lax.psum_scatter(kv, "mp", scatter_dimension=0, tiled=False)
    local_grads = jnp.concatenate([grad_q, jnp.transpose(kv)], axis=1)
    grads = lax.all_gather(local_grads, "dp", axis=0, tiled=True, axis_index_groups=Z_GROUPS)
    part = lax.dot_general(
        gathered, grads, (((0,), (0,)), ((), ())), preferred_element_type=jnp.float32
    ).astype(jnp.bfloat16)
    return part, local_grads


def whole(normed, w_query, w_key, w_value, query, key, value, grad_context):
    part, local_grads = shards(
        normed, w_query, w_key, w_value, query, key, value, grad_context
    )
    weights = jnp.concatenate([w_query, w_key, w_value], axis=1)
    total = lax.dot_general(
        local_grads, weights, (((1,), (1,)), ((), ())), preferred_element_type=jnp.float32
    ).astype(jnp.bfloat16)
    grad_input = lax.psum_scatter(total, "mp", scatter_dimension=0, tiled=True)
    weight_sum = lax.psum_scatter(
        part, "dp", scatter_dimension=0, tiled=True, axis_index_groups=Y_GROUPS
    )
    query_cols = w_query.shape[1]
    columns = w_key.shape[1]
    return (
        grad_input,
        weight_sum[:, :query_cols],
        weight_sum[:, query_cols : query_cols + columns],
        weight_sum[:, query_cols + columns :],
    )


def solution(mesh):
    placed = (
        P(("dp", "mp"), None),
        P(None, "mp"),
        P(None, "mp"),
        P(None, "mp"),
        P("dp", "mp"),
        P("dp", None),
        P("dp", None),
        P("dp", "mp"),
    )
    return jax.shard_map(
        whole,
        mesh=mesh,
        in_specs=placed,
        out_specs=(P(("dp", "mp"), None), P("dp", "mp"), P("dp", "mp"), P("dp", "mp")),
        check_vma=False,
    )
```

time: 542 us -> 317 us (0.58)
  waiting for transfers between devices: 441 us -> 231 us
  matrix products: 45.8 us -> 24.1 us
  blocking collectives: 15.8 us -> 23 us
    unnamed x6, waiting for transfers between devices: 231 us -> 14.7 us
    all_gather x1 -> x2, waiting for transfers between devices: 39.2 us -> 93.4 us  [the longest x1 50.8 us: shards(): gathered = lax.all_gather(exchanged, 'mp', axis=0, tiled=False)]
    reduce_scatter x3 -> x2, waiting for transfers between devices: 171 us -> 123 us  [the longest x1 83.9 us: whole(): grad_input = lax.psum_scatter(total, 'mp', scatter_dimension=0, tiled=True)]
    dot_general x6 -> x4, matrix products: 44.1 us -> 22.4 us  [the longest x1 13.1 us: whole(): lax.dot_general(local_grads, weights, (((1,), (1,)), ((), ())), preferred...]
    unnamed x22 -> x18, local copies, waits for them, and re-layouts: 16.5 us -> 7.94 us
    all_to_all x1, blocking collectives: 15.8 us -> 23 us  [shards(): lax.all_to_all(jnp.transpose(normed.reshape(normed.shape[0], 2, 8, -1), (...]
    transpose x0 -> x1, local copies, waits for them, and re-layouts: none -> 6.56 us  [shards(): gathered = jnp.transpose(gathered, (1, 0, 2, 3)).reshape(8 * rows, -1)]
  transfers between devices with their start and end apart: 5 -> 5, of which waited for: 5 -> 5; matrix products, arithmetic and copies ran while one was open for 11% -> 10% of each run, Pallas kernels for 0% -> 0%
where the time goes in v1:
time: 317 us; the launch traced here: 315 us
  waiting for transfers between devices  231 us (73%)
  matrix products  24.1 us (8%)
  blocking collectives  23 us (7%)
  local copies, waits for them, and re-layouts  19.8 us (6%)
  between operations  13.9 us (4%)
    reduce_scatter x1, waiting for transfers between devices, whole(): grad_input = lax.psum_scatter(total, 'mp', scatter_dimension=0, tiled=True)  83.9 us
    all_gather x1, waiting for transfers between devices, shards(): gathered = lax.all_gather(exchanged, 'mp', axis=0, tiled=False)  50.8 us
    all_gather x1, waiting for transfers between devices, shards(): lax.all_gather(local_grads, 'dp', axis=0, tiled=True, axis_index_groups=Z...  42.6 us
    reduce_scatter x1, waiting for transfers between devices, shards(): kv = lax.psum_scatter(kv, 'mp', scatter_dimension=0, tiled=False)  39.3 us
    all_to_all x1, blocking collectives, shards(): lax.all_to_all(jnp.transpose(normed.reshape(normed.shape[0], 2, 8, -1), (...  23 us
    unnamed x6, waiting for transfers between devices  14.7 us
    dot_general x1, matrix products, whole(): lax.dot_general(local_grads, weights, (((1,), (1,)), ((), ())), preferred...  13.1 us
    dot_general x1, matrix products, shards(): lax.dot_general(gathered, grads, (((0,), (0,)), ((), ())), preferred_elem...  8.49 us
  transfers between devices with their start and end apart: 5, of which 5 were waited for; matrix products, arithmetic and copies ran while one was open for 10% of the time, Pallas kernels for 0%

profile of v1, /device:TPU:1, one launch (start us, length us, event | category | flops | bytes accessed | tf_op | source)
XLA Modules:
  0.0 315.0 jit_solution(4940620076638154963)
XLA Ops:
  7.2 0.0 copy-start
  7.2 0.0 reduce-scatter.6.cloned.1.call-start
  7.3 1.2 copy.83
  8.5 1.2 copy.55
  9.7 0.0 copy-done
  9.7 0.6 fusion.36
  10.3 0.4 fusion.19
  10.7 0.5 copy-done.5
  11.2 0.4 fusion.16
  11.6 0.3 fusion.13
  12.0 0.0 copy-start.1
  12.0 0.4 fusion.18
  12.4 0.8 pad_maximum_fusion.1
  13.2 0.0 reduce-scatter.6.cloned.1.call-update
  13.2 0.0 all-gather.6.cloned.1.call-start
  13.2 0.0 copy-done.1
  13.3 0.4 reshape.47
  13.7 0.4 copy.85
  14.1 0.3 reshape.48
  14.4 23.0 %all_to_all.5 = bf16[8,24,1152]{2,1,0:T(8,128)(2,1)} all-to-all(bf16[8,24,1152]{2,1,0:T(8,128)(2,1)S(1)} %reshape.48), channel_id=1, replica_groups={{0,16,32,48,64,80,96,112},{128,144,160,176,192,208,224,240},{1,17,33,49..., dimensions={0} | all-to-all | bytes 884736 | tf_op jit(solution)/shard_map/all_to_all | solution.py:15
  37.4 0.0 all-gather.6.cloned.1.call-update
  37.4 0.0 all-gather.4.cloned.1.call-start
  37.5 0.4 fusion.15
  37.9 39.3 %reduce-scatter.6.cloned.1.call-done = bf16[1,32,384]{2,1,0:T(8,128)(2,1)} async-done(((bf16[16,32,384]{2,1,0:T(8,128)(2,1)}), bf16[1,32,384]{2,1,0:T(8,128)(2,1)}) %reduce-scatter.6.cloned.1.call-update) | async-done | bytes 24592 | tf_op jit(solution)/shard_map/reduce_scatter | solution.py:51
  77.2 1.5 pad_maximum_fusion
  78.7 0.0 all-gather.4.cloned.1.call-update
  78.7 0.0 reduce-scatter.10.cloned.1.call-start
  78.8 50.8 %all-gather.6.cloned.1.call-done = bf16[128,24,1152]{2,1,0:T(8,128)(2,1)} async-done(((bf16[8,24,1152]{2,1,0:T(8,128)(2,1)}), bf16[128,24,1152]{2,1,0:T(8,128)(2,1)}) %all-gather.6.cloned.1.call-update) | async-done | bytes 7077904 | tf_op jit(solution)/shard_map/all_gather | solution.py:21
  129.6 6.6 %copy.67 = bf16[8,16,24,1152]{3,2,1,0:T(8,128)(2,1)} copy(bf16[8,16,24,1152]{3,2,0,1:T(8,128)(2,1)} %bitcast.85) | data formatting | bytes 14155776 | tf_op jit(solution)/shard_map/transpose | solution.py:22
  136.1 42.6 %all-gather.4.cloned.1.call-done = bf16[3072,544]{0,1:T(8,128)(2,1)} async-done(((bf16[384,544]{0,1:T(8,128)(2,1)}), bf16[3072,544]{0,1:T(8,128)(2,1)}) %all-gather.4.cloned.1.call-update) | async-done | bytes 3342352 | tf_op jit(solution)/shard_map/all_gather | solution.py:53
  178.7 8.5 %fusion.6 = bf16[1152,544]{0,1:T(8,128)(2,1)S(1)} fusion(bf16[3072,544]{0,1:T(8,128)(2,1)} %all-gather.4.cloned.1.call-done, bf16[3072,1152]{1,0:T(8,128)(2,1)} %bitcast.86), kind=kOutput, calls=%fused_computation.8 | convolution fusion | flops 3850997760 | bytes 11673600 | tf_op jit(solution)/shard_map/dot_general | solution.py:54
  187.2 0.0 copy-start.2
  187.2 1.7 copy.78
  188.9 0.0 reduce-scatter.10.cloned.1.call-update
  188.9 0.2 reduce-scatter.8.cloned.1.call-start
  189.2 0.0 copy-done.2
  189.2 1.1 copy.64
  190.3 0.0 copy-done.3
  190.3 0.0 copy-start.4
  190.3 1.9 copy.65
  192.3 13.1 %convolution_convert_fusion = bf16[384,9216]{1,0:T(8,128)(2,1)} fusion(bf16[9216,16]{1,0:T(8,128)(2,1)} %copy.65, bf16[9216,16]{1,0:T(8,128)(2,1)S(1)} %copy.64, bf16[9216,512]{1,0:T(8,128)(2,1)} %param.9, bf16[384,32]{0,1:T(8,128)(2,1)S(1)} %bitcast.98, bf16[384,512]{0,1:T(8,128)(2,1)S(1)} %bitcast.89), kind=kOutput, calls=%fused_computation.1 | convolution fusion | flops 3884826624 | bytes 17522688 | tf_op jit(solution)/shard_map/dot_general | solution.py:65
  205.4 0.0 reduce-scatter.8.cloned.1.call-update
  205.4 14.7 %reduce-scatter.10.cloned.1.call-done = bf16[576,544]{1,0:T(8,128)(2,1)} async-done(((bf16[1152,544]{1,0:T(8,128)(2,1)}), bf16[576,544]{1,0:T(8,128)(2,1)}) %reduce-scatter.10.cloned.1.call-update) | async-done | bytes 626704
  220.1 1.1 fusion.35
  221.2 0.7 copy.82
  221.9 0.7 copy.81
  222.6 1.9 slice.12
  224.5 83.9 %reduce-scatter.8.cloned.1.call-done = bf16[24,9216]{1,0:T(8,128)(2,1)} async-done(((bf16[384,9216]{1,0:T(8,128)(2,1)}), bf16[24,9216]{1,0:T(8,128)(2,1)}) %reduce-scatter.8.cloned.1.call-update) | async-done | bytes 442384 | tf_op jit(solution)/shard_map/reduce_scatter | solution.py:68
  (4 shorter events, 0.0 us)
Async XLA Ops:
  7.2 2.5 copy-start
  7.2 70.0 %reduce-scatter.6.cloned.1.call-start = ((), (), s32[]{:S(2)}) async-start(), calls=%async_computation.4 | async-start | bytes 417792 | tf_op jit(solution)/shard_map/reduce_scatter | solution.py:51
  10.3 0.9 copy-start.5
  12.0 1.3 copy-start.1
  13.2 116.4 %all-gather.6.cloned.1.call-start = ((), (), s32[]{:S(2)}) async-start(), calls=%async_computation.7 | async-start | bytes 7520256 | tf_op jit(solution)/shard_map/all_gather | solution.py:21
  37.4 141.3 %all-gather.4.cloned.1.call-start = ((), (), s32[]{:S(2)}) async-start(), calls=%async_computation.6 | async-start | bytes 3760128 | tf_op jit(solution)/shard_map/all_gather | solution.py:53
  78.7 141.4 %reduce-scatter.10.cloned.1.call-start = ((), (), s32[]{:S(2)}) async-start(), calls=%async_computation.8 | async-start | bytes 2211840
  187.2 2.0 copy-start.2
  188.9 1.4 copy-start.3
  188.9 119.5 %reduce-scatter.8.cloned.1.call-start = ((), (), s32[]{:S(2)}) async-start(), calls=%async_computation.5 | async-start | bytes 7520256 | tf_op jit(solution)/shard_map/reduce_scatter | solution.py:68
  190.3 1.9 copy-start.4
Sparse Core Ops, SparseCore 0:
  13.3 63.8 reduce-scatter.5
  79.2 50.3 all-gather.5
  132.1 46.5 all-gather.3
  189.1 30.9 reduce-scatter.9
  223.3 85.1 reduce-scatter.7

commit v2 on v0

v2 whole, which is shorter than its diff:
```python
import jax
import jax.numpy as jnp
from jax import lax
from jax.experimental import pallas as pl
from jax.experimental.pallas import tpu as pltpu
from jax.sharding import PartitionSpec as P

HEAD_DIM = 256
TOK = 384
NZ = 8
CHIPS = 8
CHIP_TOK = 48
FEAT = 9216
HALF = FEAT // 2
BLOCK = 576
ZF = 2 * BLOCK
QC = 512
GC = 544
FC = 768
NCH = HALF // FC
YW = 640
MESH = pl.DeviceIdType.MESH
F32 = jnp.float32
BF16 = jnp.bfloat16
NT = (((1,), (1,)), ((), ()))


def dot(a, b):
    return jnp.dot(a, b, preferred_element_type=F32)


def dot_nt(a, b):
    return lax.dot_general(a, b, NT, preferred_element_type=F32)


def kernel(
    normed, wq_hbm, wkv, query, key, value, grad,
    out_in, out_wq, out_wkv,
    w_buf, s_buf, s_recv, t_buf, n_buf, gt_buf, g_buf, kv_buf, kv_recv, kv_all, kvg_buf,
    p_send, p_recv, r_buf, r_recv, f_send, f_buf, acc, own_buf, y_send, y_recv,
    w_sem, s_sems, a2a_ss, a2a_rs, ag_ss, ag_rs, sib_ss, sib_rs, kv_ss, kv_rs, kz_ss, kz_rs,
    cw_ss, cw_rs, cc_ss, cc_rs, p_ss, p_rs, r_ss, r_rs, f_ss, f_rs, y_sems,
):
    dp = lax.axis_index("dp")
    mp = lax.axis_index("mp")
    z = lax.rem(dp, NZ)
    y_hi = lax.div(dp, NZ)
    base = y_hi * NZ
    core = lax.rem(mp, 2)
    chip = lax.div(mp, 2)
    other = 1 - core
    sibling = (dp, chip * 2 + other)
    zhalf = lax.div(z, 4)
    y_mate = (lax.rem(dp + NZ, 2 * NZ), mp)

    def remote(src, dst, ss, rs, device):
        return pltpu.make_async_remote_copy(
            src_ref=src, dst_ref=dst, send_sem=ss, recv_sem=rs,
            device_id=device, device_id_type=MESH,
        )

    w_copy = pltpu.make_async_copy(wq_hbm, w_buf, w_sem)
    w_copy.start()

    barrier = pltpu.get_barrier_semaphore()
    for i in range(1, NZ):
        there = base + lax.rem(z + i, NZ)
        pl.semaphore_signal(barrier, inc=1, device_id=(there, mp), device_id_type=MESH)
        pl.semaphore_signal(
            barrier, inc=1, device_id=(there, chip * 2 + other), device_id_type=MESH
        )
    pl.semaphore_signal(barrier, inc=1, device_id=y_mate, device_id_type=MESH)
    for i in range(1, 2 * CHIPS):
        pl.semaphore_signal(
            barrier, inc=1, device_id=(dp, lax.rem(mp + i, 2 * CHIPS)), device_id_type=MESH
        )

    for h in range(2):
        for part in range(2):
            cols = normed[:, HALF * part + 2304 * h : HALF * part + 2304 * h + 2304].astype(F32)
            padded = jnp.concatenate([cols, jnp.zeros((8, 2304), F32)], axis=0)
            s_buf[h, :, 2304 * part : 2304 * part + 2304] = padded.astype(BF16)
    pl.semaphore_wait(barrier, 2 * (NZ - 1) + 1 + 2 * CHIPS - 1)
    s_copy = remote(s_buf.at[other], s_recv, s_sems.at[0], s_sems.at[1], sibling)
    s_copy.start()

    key_v = key[...]
    value_v = value[...]
    key_t = jnp.transpose(key_v.astype(F32)).astype(BF16)
    scale = HEAD_DIM ** (-0.5)
    causal = lax.broadcasted_iota(jnp.int32, (TOK, TOK), 0) <= lax.broadcasted_iota(
        jnp.int32, (TOK, TOK), 1
    )
    kp = None
    vp = None
    for h in range(2):
        q_h = query[:, HEAD_DIM * h : HEAD_DIM * h + HEAD_DIM]
        g_h = grad[:, HEAD_DIM * h : HEAD_DIM * h + HEAD_DIM]
        scores = jnp.where(causal, dot_nt(key_v, q_h) * scale, -jnp.inf)
        expo = jnp.exp(scores - jnp.max(scores, axis=0, keepdims=True))
        probs = expo * (1.0 / jnp.sum(expo, axis=0, keepdims=True))
        low = probs.astype(BF16)
        dprob = dot_nt(value_v, g_h)
        delta = jnp.sum(low.astype(F32) * dprob, axis=0, keepdims=True)
        dscore = (probs * (dprob - delta)).astype(BF16)
        kp_h = dot(dscore, q_h)
        vp_h = dot(low, g_h)
        kp = kp_h if kp is None else kp + kp_h
        vp = vp_h if vp is None else vp + vp_h
        gq = dot(key_t, dscore) * scale
        gt_buf[z, HEAD_DIM * h : HEAD_DIM * h + HEAD_DIM, :] = gq.astype(BF16)
        g_buf[:, HEAD_DIM * h : HEAD_DIM * h + HEAD_DIM] = jnp.transpose(gq).astype(BF16)
        if h == 0:
            s_copy.wait_recv()
            mine = s_buf[core].astype(F32)[:24]
            theirs = s_recv[...].astype(F32)[:24]
            first = jnp.where(core == 0, mine, theirs)
            second = jnp.where(core == 0, theirs, mine)
            both = jnp.concatenate([first, second], axis=0)
            for j in range(4):
                block = jnp.concatenate(
                    [
                        both[:, BLOCK * j : BLOCK * j + BLOCK],
                        both[:, 2304 + BLOCK * j : 2304 + BLOCK * j + BLOCK],
                    ],
                    axis=1,
                )
                t_buf[j] = block.astype(BF16)
            chip_rows = pl.ds(pl.multiple_of(chip * CHIP_TOK, 16), CHIP_TOK)

            def a2a(j):
                peer = 4 * core + j
                return remote(
                    t_buf.at[j], n_buf.at[z, chip_rows, :], a2a_ss.at[j], a2a_rs.at[lax.rem(z, 4)],
                    (base + peer, chip * 2 + zhalf),
                )

            def a2a_in(j):
                peer = 4 * core + j
                return remote(
                    t_buf.at[j], n_buf.at[peer, chip_rows, :], a2a_ss.at[j], a2a_rs.at[j],
                    (base + peer, chip * 2 + zhalf),
                )

            for j in range(4):
                @pl.when(4 * core + j != z)
                def _(j=j):
                    a2a(j).start()

                @pl.when(4 * core + j == z)
                def _(j=j):
                    n_buf[z, chip_rows, :] = t_buf[j]

    right = (base + lax.rem(z + 1, NZ), mp)
    left = (base + lax.rem(z + NZ - 1, NZ), mp)

    def ring(s):
        slot_r = lax.rem(z - (s - 1) + NZ, NZ)
        slot_l = lax.rem(z + (s - 1), NZ)
        if s < 4:
            src_r, src_l = gt_buf.at[slot_r], gt_buf.at[slot_l]
        else:
            src_r, src_l = gt_buf.at[slot_r, 0:256, :], gt_buf.at[slot_l, 256:512, :]
        return (
            remote(src_r, src_r, cw_ss.at[s - 1], cw_rs.at[s - 1], right),
            remote(src_l, src_l, cc_ss.at[s - 1], cc_rs.at[s - 1], left),
        )

    def ring_in(s):
        slot_r = lax.rem(z - s + NZ, NZ)
        slot_l = lax.rem(z + s, NZ)
        if s < 4:
            dst_r, dst_l = gt_buf.at[slot_r], gt_buf.at[slot_l]
        else:
            dst_r, dst_l = gt_buf.at[slot_r, 0:256, :], gt_buf.at[slot_l, 256:512, :]
        return (
            remote(dst_r, dst_r, cw_ss.at[s - 1], cw_rs.at[s - 1], right),
            remote(dst_l, dst_l, cc_ss.at[s - 1], cc_rs.at[s - 1], left),
        )

    def ring_start(s):
        for copy in ring(s):
            copy.start()

    def ring_wait(s):
        for copy in ring_in(s):
            copy.wait_recv()

    kp_t = jnp.transpose(kp * scale)
    vp_t = jnp.transpose(vp)
    kv_buf[:, 0:16, :] = kp_t.reshape(16, 16, TOK).astype(BF16)
    kv_buf[:, 16:32, :] = vp_t.reshape(16, 16, TOK).astype(BF16)

    def kv_copy(i):
        there = lax.rem(mp + i, 2 * CHIPS)
        return remote(
            kv_buf.at[there], kv_recv.at[i - 1], kv_ss.at[i - 1], kv_rs.at[i - 1], (dp, there)
        )

    for i in range(1, 2 * CHIPS):
        kv_copy(i).start()
    ring_start(1)

    def n_block(k):
        return n_buf.at[
            pl.ds(4 * core, 4), pl.ds(pl.multiple_of(k * CHIP_TOK, 16), CHIP_TOK), :
        ]

    def n_block_in(k):
        return n_buf.at[
            pl.ds(4 * other, 4), pl.ds(pl.multiple_of(k * CHIP_TOK, 16), CHIP_TOK), :
        ]

    def ag(i):
        there = lax.rem(chip + i, CHIPS)
        return remote(
            n_block(chip), n_block(chip), ag_ss.at[i - 1], ag_rs.at[i - 1],
            (dp, there * 2 + core),
        )

    def ag_in(i):
        k = lax.rem(chip - i + CHIPS, CHIPS)
        return remote(n_block(k), n_block(k), ag_ss.at[i - 1], ag_rs.at[i - 1], sibling)

    def sib(i):
        k = lax.rem(chip - i + CHIPS, CHIPS)
        return remote(n_block(k), n_block(k), sib_ss.at[i], sib_rs.at[i], sibling)

    def sib_in(i):
        k = lax.rem(chip - i + CHIPS, CHIPS)
        return remote(n_block_in(k), n_block_in(k), sib_ss.at[i], sib_rs.at[i], sibling)

    for j in range(4):
        @pl.when(4 * core + j != z)
        def _(j=j):
            a2a_in(j).wait_recv()
    for i in range(1, CHIPS):
        ag(i).start()
    sib(0).start()

    for i in range(1, 2 * CHIPS):
        kv_copy(i).wait_recv()
    kv_sum = kv_buf[mp].astype(F32)
    for i in range(15):
        kv_sum = kv_sum + kv_recv[i].astype(F32)
    kv_all[z] = kv_sum.astype(BF16)
    kvg_buf[...] = jnp.transpose(kv_sum).astype(BF16)

    def kz(i):
        return remote(
            kv_all.at[z], kv_all.at[z], kz_ss.at[i - 1], kz_rs.at[i - 1],
            (base + lax.rem(z + i, NZ), mp),
        )

    def kz_in(i):
        slot = lax.rem(z - i + NZ, NZ)
        return remote(
            kv_all.at[slot], kv_all.at[slot], kz_ss.at[i - 1], kz_rs.at[i - 1],
            (base + lax.rem(z + i, NZ), mp),
        )

    for i in range(1, NZ):
        kz(i).start()

    w_copy.wait()

    def partial(first):
        first = pl.multiple_of(first, FC)
        total = dot_nt(g_buf[...], w_buf[pl.ds(first, FC), :])
        return total + dot(kvg_buf[...], wkv[:, pl.ds(first, FC)])

    def p_copy(j):
        return remote(p_send.at[j], p_recv.at[j], p_ss.at[j], p_rs.at[j], sibling)

    def sib_half(j, carry):
        p_send[j] = partial(other * HALF + j * FC).astype(BF16)
        p_copy(j).start()
        return carry

    lax.fori_loop(0, NCH, sib_half, 0)
    ring_wait(1)
    ring_start(2)

    def r_copy(i, j):
        there = lax.rem(chip + i, CHIPS)
        return remote(
            r_buf.at[j, pl.ds(pl.multiple_of(there * CHIP_TOK, 16), CHIP_TOK), :],
            r_recv.at[i - 1, j], r_ss.at[i - 1, j], r_rs.at[i - 1, j],
            (dp, there * 2 + core),
        )

    def own_half(j, carry):
        total = partial(core * HALF + j * FC)
        p_copy(j).wait_recv()
        r_buf[j] = (total + p_recv[j].astype(F32)).astype(BF16)
        for i in range(1, CHIPS):
            r_copy(i, j).start()
        return carry

    lax.fori_loop(0, NCH, own_half, 0)
    ring_wait(2)
    ring_start(3)
    for i in range(1, 4):
        ag_in(i).wait_recv()
        sib(i).start()
    ring_wait(3)
    ring_start(4)
    for i in range(4, CHIPS):
        ag_in(i).wait_recv()
        sib(i).start()
    for i in range(1, NZ):
        kz_in(i).wait_recv()
    ring_wait(4)
    for i in range(CHIPS):
        sib_in(i).wait_recv()

    acc[...] = jnp.zeros_like(acc)

    def wgrad(p, carry):
        top = jnp.concatenate([gt_buf[2 * p], gt_buf[2 * p + 1]], axis=1)
        low = jnp.concatenate([kv_all[2 * p], kv_all[2 * p + 1]], axis=1)
        for c in range(3):
            cols = slice(TOK * c, TOK * c + TOK)
            rhs = jnp.concatenate([n_buf[2 * p, :, cols], n_buf[2 * p + 1, :, cols]], axis=0)
            acc[0:QC, cols] += dot(top, rhs)
            acc[QC:GC, cols] += dot(low, rhs)
        return carry

    lax.fori_loop(0, NZ // 2, wgrad, 0)

    def split(r, carry):
        rows = pl.ds(pl.multiple_of(r * 32, 32), 32)
        here = acc[rows, :]
        lower = here[:, 0:YW]
        upper = pltpu.roll(here, BLOCK, 1)[:, 0:YW]
        y_send[rows, :] = jnp.where(y_hi == 0, upper, lower).astype(BF16)
        own_buf[rows, :] = jnp.where(y_hi == 0, lower, upper)
        return carry

    lax.fori_loop(0, GC // 32, split, 0)
    y_copy = remote(y_send, y_recv, y_sems.at[0], y_sems.at[1], y_mate)
    y_copy.start()

    def f_copy(j):
        return remote(f_send.at[j], f_buf.at[core, j], f_ss.at[j], f_rs.at[j], sibling)

    def f_in(j):
        return remote(f_send.at[j], f_buf.at[other, j], f_ss.at[j], f_rs.at[j], sibling)

    def finish(j, carry):
        rows = pl.ds(pl.multiple_of(chip * CHIP_TOK, 16), CHIP_TOK)
        total = r_buf[j, rows, :].astype(F32)
        for i in range(1, CHIPS):
            r_copy(i, j).wait_recv()
            total = total + r_recv[i - 1, j].astype(F32)
        low, high = total[0:24], total[24:48]
        pad = jnp.zeros((8, FC), F32)
        mine = jnp.where(core == 0, low, high)
        theirs = jnp.where(core == 0, high, low)
        f_buf[core, j] = jnp.concatenate([mine, pad], axis=0).astype(BF16)
        f_send[j] = jnp.concatenate([theirs, pad], axis=0).astype(BF16)
        f_copy(j).start()
        return carry

    lax.fori_loop(0, NCH, finish, 0)
    for j in range(NCH):
        f_in(j).wait_recv()
    for h in range(2):
        for j in range(NCH):
            out_in[:, HALF * h + FC * j : HALF * h + FC * j + FC] = f_buf[h, j].astype(F32)[
                0:24
            ].astype(BF16)

    y_copy.wait_recv()
    for c in range(4):
        rows = slice(128 * c, 128 * c + 128)
        total = own_buf[rows, :] + y_recv[rows, :].astype(F32)
        out_wq[:, rows] = jnp.transpose(total)[0:BLOCK].astype(BF16)
    total = own_buf[QC:GC, :] + y_recv[QC:GC, :].astype(F32)
    out_wkv[...] = total[:, 0:BLOCK].astype(BF16)

    s_copy.wait_send()
    for j in range(4):
        @pl.when(4 * core + j != z)
        def _(j=j):
            a2a(j).wait_send()
    for i in range(1, 2 * CHIPS):
        kv_copy(i).wait_send()
    for i in range(1, NZ):
        kz(i).wait_send()
    for i in range(1, CHIPS):
        ag(i).wait_send()
    for i in range(CHIPS):
        sib(i).wait_send()
    for s in range(1, 5):
        for copy in ring(s):
            copy.wait_send()

    def drain(j, carry):
        p_copy(j).wait_send()
        f_copy(j).wait_send()
        for i in range(1, CHIPS):
            r_copy(i, j).wait_send()
        return carry

    lax.fori_loop(0, NCH, drain, 0)
    y_copy.wait_send()


def shards(normed, w_query, w_key, w_value, query, key, value, grad_context):
    wkv = jnp.concatenate([jnp.transpose(w_key), jnp.transpose(w_value)], axis=0)
    vmem = pl.BlockSpec(memory_space=pltpu.VMEM)
    dma = pltpu.SemaphoreType.DMA
    grad_input, grad_wq, grad_wkv = pl.pallas_call(
        kernel,
        out_shape=(
            jax.ShapeDtypeStruct((24, FEAT), BF16),
            jax.ShapeDtypeStruct((BLOCK, QC), BF16),
            jax.ShapeDtypeStruct((32, BLOCK), BF16),
        ),
        in_specs=[vmem, pl.BlockSpec(memory_space=pl.ANY), vmem, vmem, vmem, vmem, vmem],
        out_specs=(vmem, vmem, vmem),
        scratch_shapes=[
            pltpu.VMEM((FEAT, QC), BF16),
            pltpu.VMEM((2, 32, HALF), BF16),
            pltpu.VMEM((32, HALF), BF16),
            pltpu.VMEM((4, CHIP_TOK, ZF), BF16),
            pltpu.VMEM((NZ, TOK, ZF), BF16),
            pltpu.VMEM((NZ, QC, TOK), BF16),
            pltpu.VMEM((TOK, QC), BF16),
            pltpu.VMEM((16, 32, TOK), BF16),
            pltpu.VMEM((15, 32, TOK), BF16),
            pltpu.VMEM((NZ, 32, TOK), BF16),
            pltpu.VMEM((TOK, 32), BF16),
            pltpu.VMEM((NCH, TOK, FC), BF16),
            pltpu.VMEM((NCH, TOK, FC), BF16),
            pltpu.VMEM((NCH, TOK, FC), BF16),
            pltpu.VMEM((CHIPS - 1, NCH, CHIP_TOK, FC), BF16),
            pltpu.VMEM((NCH, 32, FC), BF16),
            pltpu.VMEM((2, NCH, 32, FC), BF16),
            pltpu.VMEM((GC, ZF), F32),
            pltpu.VMEM((GC, YW), F32),
            pltpu.VMEM((GC, YW), BF16),
            pltpu.VMEM((GC, YW), BF16),
            dma,
            dma((2,)),
            dma((4,)), dma((4,)),
            dma((7,)), dma((7,)),
            dma((8,)), dma((8,)),
            dma((15,)), dma((15,)),
            dma((7,)), dma((7,)),
            dma((4,)), dma((4,)), dma((4,)), dma((4,)),
            dma((NCH,)), dma((NCH,)),
            dma((7, NCH)), dma((7, NCH)),
            dma((NCH,)), dma((NCH,)),
            dma((2,)),
        ],
        compiler_params=pltpu.CompilerParams(
            collective_id=0, has_side_effects=True, vmem_limit_bytes=60 * 1024 * 1024
        ),
    )(normed, w_query, wkv, query, key, value, grad_context)
    return grad_input, grad_wq, jnp.transpose(grad_wkv[0:16]), jnp.transpose(grad_wkv[16:32])


def solution(mesh):
    placed = (
        P(("dp", "mp"), None),
        P(None, "mp"),
        P(None, "mp"),
        P(None, "mp"),
        P("dp", "mp"),
        P("dp", None),
        P("dp", None),
        P("dp", "mp"),
    )
    return jax.shard_map(
        shards,
        mesh=mesh,
        in_specs=placed,
        out_specs=(P(("dp", "mp"), None), P("dp", "mp"), P("dp", "mp"), P("dp", "mp")),
        check_vma=False,
    )
```

time: 542 us -> 139 us (0.26)
  the two profiles are of different devices: /device:TPU:1 before, /device:TPU:77 now
where the time goes in v2:
time: 139 us
  Pallas kernels  132 us (95%)
  local copies, waits for them, and re-layouts  4.04 us (3%)
  other arithmetic  1.9 us (1%)
    pallas_call x1, Pallas kernels, shards(): pl.pallas_call(kernel, out_shape=(jax.ShapeDtypeStruct((24, FEAT), BF16),...  132 us

profile of v2, /device:TPU:77, one launch (start us, length us, event | category | flops | bytes accessed | tf_op | source)
XLA Modules:
  0.0 139.0 jit_solution(6681892432213093256)
XLA Ops:
  0.6 1.9 %pad_maximum_fusion.wkv = bf16[32,9216]{1,0:T(8,128)(2,1)} fusion(bf16[16,9216]{1,0:T(8,128)(2,1)} %bitcast.6, bf16[16,9216]{1,0:T(8,128)(2,1)} %bitcast.7), kind=kLoop, calls=%fused_computation | loop fusion | flops 1179648 | bytes 1179648 | tf_op jit(solution)/shard_map/concatenate | solution.py:411
  2.5 132.4 %shard_map.111 = (bf16[24,9216]{1,0:T(8,128)(2,1)}, bf16[576,512]{1,0:T(8,128)(2,1)}, bf16[32,576]{1,0:T(8,128)(2,1)}) custom-call(bf16[24,9216]{1,0:T(8,128)(2,1)} %normed.1, bf16[9216,512]{1,0:T(8,128)(2,1)} %wq_hbm.1, bf16[32,9216]{1,0:T(8,128)(2,1)} %pad_maximum_fusion.wkv, bf16[384,512]{1,0:T(8,128)(2,1)} %query.1, bf16[384,256]{1,0:T(8,128)(2,1)} %key.1, ...), custom_call_target="tpu_custom_call" | custom-call | tf_op jit(solution)/shard_map/pallas_call | solution.py:414
  135.0 0.0 copy-start
  135.0 1.4 %slice_bitcast_fusion = (bf16[576,16]{0,1:T(8,128)(2,1)}, bf16[576,16]{0,1:T(8,128)(2,1)}) fusion(bf16[32,576]{1,0:T(8,128)(2,1)} %get-tuple-element.9), kind=kLoop, calls=%fused_computation.1 | loop fusion | bytes 73728 | tf_op jit(solution)/shard_map/transpose | solution.py:462
  136.4 1.8 %copy.14 = bf16[24,9216]{1,0:T(8,128)(2,1)} copy(bf16[24,9216]{1,0:T(8,128)(2,1)} %get-tuple-element.16) | data formatting | bytes 884736
  138.2 0.0 copy-done
  138.2 0.8 copy.15
Async XLA Ops:
  135.0 3.2 %copy-start = (bf16[576,512]{1,0:T(8,128)(2,1)S(1)}, bf16[576,512]{1,0:T(8,128)(2,1)}, u32[]{:S(2)}) copy-start(bf16[576,512]{1,0:T(8,128)(2,1)} %get-tuple-element.17) | copy-start | bytes 1769476

commit v3 on v2

--- a/solution.py
+++ b/solution.py
@@ -34,12 +34,15 @@
 
 
 def kernel(
-    normed, wq_hbm, wkv, query, key, value, grad,
-    out_in, out_wq, out_wkv,
-    w_buf, s_buf, s_recv, t_buf, n_buf, gt_buf, g_buf, kv_buf, kv_recv, kv_all, kvg_buf,
-    p_send, p_recv, r_buf, r_recv, f_send, f_buf, acc, own_buf, y_send, y_recv,
-    w_sem, s_sems, a2a_ss, a2a_rs, ag_ss, ag_rs, sib_ss, sib_rs, kv_ss, kv_rs, kz_ss, kz_rs,
-    cw_ss, cw_rs, cc_ss, cc_rs, p_ss, p_rs, r_ss, r_rs, f_ss, f_rs, y_sems,
+    normed, wq_hbm, wk_t, wv_t, query, key, value, grad,
+    out_in, out_wq, out_wk, out_wv,
+    w_buf, wkv, s_buf, s_recv, t_buf, n_buf, gt_buf, g_buf, kv_buf, kv_recv, kv_all, kvg_buf,
+    p_send, p_recv, r_buf, rx_recv, rx_send, rx_last, ry_recv, ry_last, f_send, f_buf,
+    acc, own_buf, own_kv, y_send, y_recv, ykv_send, ykv_recv,
+    w_sems, s_sems, a2a_ss, a2a_rs, agy_ss, agy_rs, agx_ss, agx_rs, agd_ss, agd_rs,
+    sib_ss, sib_rs, kv_ss, kv_rs, kz_ss, kz_rs,
+    cw_ss, cw_rs, cc_ss, cc_rs, p_ss, p_rs,
+    rx_ss, rx_rs, rxy_ss, rxy_rs, ry_ss, ry_rs, ryx_ss, ryx_rs, f_ss, f_rs, y_ss, y_rs,
 ):
     dp = lax.axis_index("dp")
     mp = lax.axis_index("mp")
@@ -51,6 +54,9 @@
     other = 1 - core
     sibling = (dp, chip * 2 + other)
     zhalf = lax.div(z, 4)
+    x = lax.div(chip, 2)
+    y_lo = lax.rem(chip, 2)
+    y_chip = chip + 1 - 2 * y_lo
     y_mate = (lax.rem(dp + NZ, 2 * NZ), mp)
 
     def remote(src, dst, ss, rs, device):
@@ -59,8 +65,16 @@
             device_id=device, device_id_type=MESH,
         )
 
-    w_copy = pltpu.make_async_copy(wq_hbm, w_buf, w_sem)
-    w_copy.start()
+    def w_copy(half, j):
+        rows = pl.ds(pl.multiple_of((half * NCH + j) * FC, FC), FC)
+        return pltpu.make_async_copy(
+            wq_hbm.at[rows, :], w_buf.at[rows, :], w_sems.at[half * NCH + j]
+        )
+
+    for j in range(NCH):
+        w_copy(other, j).start()
+    for j in range(NCH):
+        w_copy(core, j).start()
 
     barrier = pltpu.get_barrier_semaphore()
     for i in range(1, NZ):
@@ -75,6 +89,8 @@
             barrier, inc=1, device_id=(dp, lax.rem(mp + i, 2 * CHIPS)), device_id_type=MESH
         )
 
+    wkv[0:16, :] = wk_t[...]
+    wkv[16:32, :] = wv_t[...]
     for h in range(2):
         for part in range(2):
             cols = normed[:, HALF * part + 2304 * h : HALF * part + 2304 * h + 2304].astype(F32)
@@ -201,42 +217,88 @@
         kv_copy(i).start()
     ring_start(1)
 
-    def n_block(k):
-        return n_buf.at[
-            pl.ds(4 * core, 4), pl.ds(pl.multiple_of(k * CHIP_TOK, 16), CHIP_TOK), :
-        ]
-
-    def n_block_in(k):
-        return n_buf.at[
-            pl.ds(4 * other, 4), pl.ds(pl.multiple_of(k * CHIP_TOK, 16), CHIP_TOK), :
-        ]
-
-    def ag(i):
-        there = lax.rem(chip + i, CHIPS)
-        return remote(
-            n_block(chip), n_block(chip), ag_ss.at[i - 1], ag_rs.at[i - 1],
-            (dp, there * 2 + core),
-        )
-
-    def ag_in(i):
-        k = lax.rem(chip - i + CHIPS, CHIPS)
-        return remote(n_block(k), n_block(k), ag_ss.at[i - 1], ag_rs.at[i - 1], sibling)
+    def n_rows(k):
+        return pl.ds(pl.multiple_of(k * CHIP_TOK, 16), CHIP_TOK)
+
+    def piece(n, k):
+        return n_buf.at[4 * core + lax.rem(z + n, 4), n_rows(k), :]
+
+    def x_chip(d):
+        return lax.rem(x + d, 4) * 2 + y_lo
+
+    def x_from(d):
+        return lax.rem(x + 4 - d, 4) * 2 + y_lo
+
+    def ag_y(n):
+        return remote(
+            piece(n, chip), piece(n, chip), agy_ss.at[n], agy_rs.at[n], (dp, y_chip * 2 + core)
+        )
+
+    def ag_x(n, d):
+        return remote(
+            piece(n, chip), piece(n, chip), agx_ss.at[n, d - 1], agx_rs.at[n, d - 1],
+            (dp, x_chip(d) * 2 + core),
+        )
+
+    def ag_d(n, d):
+        if n % 2 == 0:
+            k, device = y_chip, (dp, x_chip(d) * 2 + core)
+        else:
+            k, device = x_from(d), (dp, y_chip * 2 + core)
+        return remote(piece(n, k), piece(n, k), agd_ss.at[n, d - 1], agd_rs.at[n, d - 1], device)
+
+    def n_block(half, k):
+        return n_buf.at[pl.ds(4 * half, 4), n_rows(k), :]
+
+    def sib_chip(i):
+        if i == 0:
+            return chip
+        if i == 1:
+            return y_chip
+        k = x_from((i - 2) % 3 + 1)
+        return k if i < 5 else k + 1 - 2 * y_lo
 
     def sib(i):
-        k = lax.rem(chip - i + CHIPS, CHIPS)
-        return remote(n_block(k), n_block(k), sib_ss.at[i], sib_rs.at[i], sibling)
+        block = n_block(core, sib_chip(i))
+        return remote(block, block, sib_ss.at[i], sib_rs.at[i], sibling)
 
     def sib_in(i):
-        k = lax.rem(chip - i + CHIPS, CHIPS)
-        return remote(n_block_in(k), n_block_in(k), sib_ss.at[i], sib_rs.at[i], sibling)
-
-    for j in range(4):
+        block = n_block(other, sib_chip(i))
+        return remote(block, block, sib_ss.at[i], sib_rs.at[i], sibling)
+
+    def ag_first(n):
+        j = lax.rem(z + n, 4)
+
         @pl.when(4 * core + j != z)
-        def _(j=j):
+        def _():
             a2a_in(j).wait_recv()
-    for i in range(1, CHIPS):
-        ag(i).start()
-    sib(0).start()
+
+        ag_y(n).start()
+        for d in (1, 3, 2):
+            ag_x(n, d).start()
+
+    def ag_second(n):
+        if n % 2 == 0:
+            ag_y(n).wait_recv()
+            for d in (1, 3, 2):
+                ag_d(n, d).start()
+        else:
+            for d in (1, 3, 2):
+                ag_x(n, d).wait_recv()
+                ag_d(n, d).start()
+
+    def ag_last():
+        for n in (1, 3):
+            ag_y(n).wait_recv()
+        sib(1).start()
+        for d in (1, 3, 2):
+            for n in (0, 2):
+                ag_x(n, d).wait_recv()
+            sib(1 + d).start()
+        for d in (1, 3, 2):
+            for n in range(4):
+                ag_d(n, d).wait_recv()
+            sib(4 + d).start()
 
     for i in range(1, 2 * CHIPS):
         kv_copy(i).wait_recv()
@@ -262,97 +324,86 @@
     for i in range(1, NZ):
         kz(i).start()
 
-    w_copy.wait()
-
-    def partial(first):
-        first = pl.multiple_of(first, FC)
+    def partial(half, j):
+        first = pl.multiple_of((half * NCH + j) * FC, FC)
+        w_copy(half, j).wait()
         total = dot_nt(g_buf[...], w_buf[pl.ds(first, FC), :])
         return total + dot(kvg_buf[...], wkv[:, pl.ds(first, FC)])
 
     def p_copy(j):
         return remote(p_send.at[j], p_recv.at[j], p_ss.at[j], p_rs.at[j], sibling)
 
-    def sib_half(j, carry):
-        p_send[j] = partial(other * HALF + j * FC).astype(BF16)
+    def sib_half(j):
+        p_send[j] = partial(other, j).astype(BF16)
         p_copy(j).start()
-        return carry
-
-    lax.fori_loop(0, NCH, sib_half, 0)
-    ring_wait(1)
-    ring_start(2)
-
-    def r_copy(i, j):
-        there = lax.rem(chip + i, CHIPS)
-        return remote(
-            r_buf.at[j, pl.ds(pl.multiple_of(there * CHIP_TOK, 16), CHIP_TOK), :],
-            r_recv.at[i - 1, j], r_ss.at[i - 1, j], r_rs.at[i - 1, j],
-            (dp, there * 2 + core),
-        )
-
-    def own_half(j, carry):
-        total = partial(core * HALF + j * FC)
+
+    def rx_copy(j, d):
+        n = 2 * (j // 3) + j % 3 - 1
+        return remote(
+            r_buf.at[j, lax.rem(x + d, 4)], rx_recv.at[n, d - 1],
+            rx_ss.at[n, d - 1], rx_rs.at[n, d - 1], (dp, x_chip(d) * 2 + core),
+        )
+
+    def rxy_copy(j):
+        n = 2 * (j // 3) + j % 3 - 1
+        return remote(
+            rx_send.at[n], rx_last.at[n], rxy_ss.at[n], rxy_rs.at[n], (dp, y_chip * 2 + core)
+        )
+
+    def ry_copy(j):
+        return remote(
+            r_buf.at[j, :, 1 - y_lo], ry_recv.at[j // 3], ry_ss.at[j // 3], ry_rs.at[j // 3],
+            (dp, y_chip * 2 + core),
+        )
+
+    def ryx_copy(j, d):
+        return remote(
+            r_buf.at[j, lax.rem(x + d, 4), y_lo], ry_last.at[j // 3, d - 1],
+            ryx_ss.at[j // 3, d - 1], ryx_rs.at[j // 3, d - 1], (dp, x_chip(d) * 2 + core),
+        )
+
+    def own_half(j):
+        total = partial(core, j)
         p_copy(j).wait_recv()
-        r_buf[j] = (total + p_recv[j].astype(F32)).astype(BF16)
-        for i in range(1, CHIPS):
-            r_copy(i, j).start()
-        return carry
-
-    lax.fori_loop(0, NCH, own_half, 0)
-    ring_wait(2)
-    ring_start(3)
-    for i in range(1, 4):
-        ag_in(i).wait_recv()
-        sib(i).start()
-    ring_wait(3)
-    ring_start(4)
-    for i in range(4, CHIPS):
-        ag_in(i).wait_recv()
-        sib(i).start()
-    for i in range(1, NZ):
-        kz_in(i).wait_recv()
-    ring_wait(4)
-    for i in range(CHIPS):
-        sib_in(i).wait_recv()
-
-    acc[...] = jnp.zeros_like(acc)
-
-    def wgrad(p, carry):
-        top = jnp.concatenate([gt_buf[2 * p], gt_buf[2 * p + 1]], axis=1)
-        low = jnp.concatenate([kv_all[2 * p], kv_all[2 * p + 1]], axis=1)
-        for c in range(3):
-            cols = slice(TOK * c, TOK * c + TOK)
-            rhs = jnp.concatenate([n_buf[2 * p, :, cols], n_buf[2 * p + 1, :, cols]], axis=0)
-            acc[0:QC, cols] += dot(top, rhs)
-            acc[QC:GC, cols] += dot(low, rhs)
-        return carry
-
-    lax.fori_loop(0, NZ // 2, wgrad, 0)
-
-    def split(r, carry):
-        rows = pl.ds(pl.multiple_of(r * 32, 32), 32)
-        here = acc[rows, :]
-        lower = here[:, 0:YW]
-        upper = pltpu.roll(here, BLOCK, 1)[:, 0:YW]
-        y_send[rows, :] = jnp.where(y_hi == 0, upper, lower).astype(BF16)
-        own_buf[rows, :] = jnp.where(y_hi == 0, lower, upper)
-        return carry
-
-    lax.fori_loop(0, GC // 32, split, 0)
-    y_copy = remote(y_send, y_recv, y_sems.at[0], y_sems.at[1], y_mate)
-    y_copy.start()
-
-    def f_copy(j):
-        return remote(f_send.at[j], f_buf.at[core, j], f_ss.at[j], f_rs.at[j], sibling)
-
-    def f_in(j):
-        return remote(f_send.at[j], f_buf.at[other, j], f_ss.at[j], f_rs.at[j], sibling)
-
-    def finish(j, carry):
-        rows = pl.ds(pl.multiple_of(chip * CHIP_TOK, 16), CHIP_TOK)
-        total = r_buf[j, rows, :].astype(F32)
-        for i in range(1, CHIPS):
-            r_copy(i, j).wait_recv()
-            total = total + r_recv[i - 1, j].astype(F32)
+        total = (total + p_recv[j].astype(F32)).astype(BF16)
+        r_buf[j] = total.reshape(4, 2, CHIP_TOK, FC)
+        if j % 3 == 0:
+            ry_copy(j).start()
+        else:
+            for d in (1, 3, 2):
+                rx_copy(j, d).start()
+
+    def rs_second(j):
+        if j % 3 == 0:
+            ry_copy(j).wait_recv()
+            for k in range(4):
+                r_buf[j, k, y_lo] = (
+                    r_buf[j, k, y_lo].astype(F32) + ry_recv[j // 3, k].astype(F32)
+                ).astype(BF16)
+            for d in (1, 3, 2):
+                ryx_copy(j, d).start()
+        else:
+            n = 2 * (j // 3) + j % 3 - 1
+            for d in range(1, 4):
+                rx_copy(j, d).wait_recv()
+            out = r_buf[j, x, 1 - y_lo].astype(F32)
+            for d in range(3):
+                out = out + rx_recv[n, d, 1 - y_lo].astype(F32)
+            rx_send[n] = out.astype(BF16)
+            rxy_copy(j).start()
+
+    def rs_last(j):
+        total = r_buf[j, x, y_lo].astype(F32)
+        if j % 3 == 0:
+            for d in range(1, 4):
+                ryx_copy(j, d).wait_recv()
+                total = total + ry_last[j // 3, d - 1].astype(F32)
+        else:
+            n = 2 * (j // 3) + j % 3 - 1
+            for d in range(3):
+                total = total + rx_recv[n, d, y_lo].astype(F32)
+            rxy_copy(j).wait_recv()
+            total = total + rx_last[n].astype(F32)
         low, high = total[0:24], total[24:48]
         pad = jnp.zeros((8, FC), F32)
         mine = jnp.where(core == 0, low, high)
@@ -360,9 +411,97 @@
         f_buf[core, j] = jnp.concatenate([mine, pad], axis=0).astype(BF16)
         f_send[j] = jnp.concatenate([theirs, pad], axis=0).astype(BF16)
         f_copy(j).start()
-        return carry
-
-    lax.fori_loop(0, NCH, finish, 0)
+
+    def f_copy(j):
+        return remote(f_send.at[j], f_buf.at[core, j], f_ss.at[j], f_rs.at[j], sibling)
+
+    def f_in(j):
+        return remote(f_send.at[j], f_buf.at[other, j], f_ss.at[j], f_rs.at[j], sibling)
+
+    def wgrad(za, zb, top_rows, with_kv):
+        top = jnp.concatenate([gt_buf[za, top_rows, :], gt_buf[zb, top_rows, :]], axis=1)
+        low = jnp.concatenate([kv_all[za], kv_all[zb]], axis=1)
+        for c in range(3):
+            cols = slice(TOK * c, TOK * c + TOK)
+            rhs = jnp.concatenate([n_buf[za, :, cols], n_buf[zb, :, cols]], axis=0)
+            acc[top_rows, cols] += dot(top, rhs)
+            if with_kv:
+                acc[QC:GC, cols] += dot(low, rhs)
+
+    def wgrad_pair(s):
+        wgrad(lax.rem(z + NZ - s, NZ), lax.rem(z + s, NZ), slice(0, QC), True)
+
+    def y_copy(r):
+        cols = slice(256 * r, 256 * r + 256)
+        return remote(y_send.at[:, cols], y_recv.at[:, cols], y_ss.at[r], y_rs.at[r], y_mate)
+
+    def ykv_copy():
+        return remote(ykv_send, ykv_recv, y_ss.at[2], y_rs.at[2], y_mate)
+
+    def halves(rows):
+        here = acc[rows, :]
+        lower = here[:, 0:YW]
+        upper = pltpu.roll(here, BLOCK, 1)[:, 0:YW]
+        return jnp.where(y_hi == 0, lower, upper), jnp.where(y_hi == 0, upper, lower)
+
+    acc[...] = jnp.zeros_like(acc)
+    sib_half(0)
+    ag_first(0)
+    sib_half(1)
+    sib_half(2)
+    ag_first(1)
+    sib_half(3)
+    ag_first(2)
+    sib_half(4)
+    sib_half(5)
+    ag_first(3)
+    sib(0).start()
+    ag_second(0)
+    ring_wait(1)
+    ring_start(2)
+    ag_second(1)
+    own_half(0)
+    own_half(1)
+    ag_second(2)
+    ag_second(3)
+    own_half(2)
+    ring_wait(2)
+    ring_start(3)
+    own_half(3)
+    own_half(4)
+    own_half(5)
+    rs_second(0)
+    ag_last()
+    ring_wait(3)
+    ring_start(4)
+    for i in range(1, NZ):
+        kz_in(i).wait_recv()
+    for i in range(CHIPS):
+        sib_in(i).wait_recv()
+    wgrad_pair(1)
+    rs_second(1)
+    wgrad_pair(2)
+    rs_second(2)
+    rs_second(3)
+    wgrad_pair(3)
+    ring_wait(4)
+    for r in range(2):
+        rows = slice(256 * r, 256 * r + 256)
+        wgrad(z, lax.rem(z + 4, NZ), rows, r == 1)
+        for q in range(2):
+            quarter = slice(256 * r + 128 * q, 256 * r + 128 * q + 128)
+            mine, theirs = halves(quarter)
+            y_send[:, quarter] = jnp.transpose(theirs)[0:BLOCK].astype(BF16)
+            own_buf[:, quarter] = jnp.transpose(mine)[0:BLOCK]
+        y_copy(r).start()
+    mine, theirs = halves(slice(QC, GC))
+    own_kv[...] = mine
+    ykv_send[...] = theirs.astype(BF16)
+    ykv_copy().start()
+    rs_second(4)
+    rs_second(5)
+    for j in range(NCH):
+        rs_last(j)
     for j in range(NCH):
         f_in(j).wait_recv()
     for h in range(2):
@@ -370,14 +509,14 @@
             out_in[:, HALF * h + FC * j : HALF * h + FC * j + FC] = f_buf[h, j].astype(F32)[
                 0:24
             ].astype(BF16)
-
-    y_copy.wait_recv()
-    for c in range(4):
-        rows = slice(128 * c, 128 * c + 128)
-        total = own_buf[rows, :] + y_recv[rows, :].astype(F32)
-        out_wq[:, rows] = jnp.transpose(total)[0:BLOCK].astype(BF16)
-    total = own_buf[QC:GC, :] + y_recv[QC:GC, :].astype(F32)
-    out_wkv[...] = total[:, 0:BLOCK].astype(BF16)
+    for r in range(2):
+        y_copy(r).wait_recv()
+        cols = slice(256 * r, 256 * r + 256)
+        out_wq[:, cols] = (own_buf[:, cols] + y_recv[:, cols].astype(F32)).astype(BF16)
+    ykv_copy().wait_recv()
+    total = (own_kv[...] + ykv_recv[...].astype(F32))[:, 0:BLOCK].astype(BF16)
+    out_wk[...] = total[0:16]
+    out_wv[...] = total[16:32]
 
     s_copy.wait_send()
     for j in range(4):
@@ -388,40 +527,48 @@
         kv_copy(i).wait_send()
     for i in range(1, NZ):
         kz(i).wait_send()
-    for i in range(1, CHIPS):
-        ag(i).wait_send()
+    for n in range(4):
+        ag_y(n).wait_send()
+        for d in range(1, 4):
+            ag_x(n, d).wait_send()
+            ag_d(n, d).wait_send()
     for i in range(CHIPS):
         sib(i).wait_send()
     for s in range(1, 5):
         for copy in ring(s):
             copy.wait_send()
-
-    def drain(j, carry):
+    for j in range(NCH):
         p_copy(j).wait_send()
         f_copy(j).wait_send()
-        for i in range(1, CHIPS):
-            r_copy(i, j).wait_send()
-        return carry
-
-    lax.fori_loop(0, NCH, drain, 0)
-    y_copy.wait_send()
+        if j % 3 == 0:
+            ry_copy(j).wait_send()
+            for d in range(1, 4):
+                ryx_copy(j, d).wait_send()
+        else:
+            for d in range(1, 4):
+                rx_copy(j, d).wait_send()
+            rxy_copy(j).wait_send()
+    for r in range(2):
+        y_copy(r).wait_send()
+    ykv_copy().wait_send()
 
 
 def shards(normed, w_query, w_key, w_value, query, key, value, grad_context):
-    wkv = jnp.concatenate([jnp.transpose(w_key), jnp.transpose(w_value)], axis=0)
     vmem = pl.BlockSpec(memory_space=pltpu.VMEM)
     dma = pltpu.SemaphoreType.DMA
-    grad_input, grad_wq, grad_wkv = pl.pallas_call(
+    grad_input, grad_wq, grad_wk, grad_wv = pl.pallas_call(
         kernel,
         out_shape=(
             jax.ShapeDtypeStruct((24, FEAT), BF16),
             jax.ShapeDtypeStruct((BLOCK, QC), BF16),
-            jax.ShapeDtypeStruct((32, BLOCK), BF16),
+            jax.ShapeDtypeStruct((16, BLOCK), BF16),
+            jax.ShapeDtypeStruct((16, BLOCK), BF16),
         ),
-        in_specs=[vmem, pl.BlockSpec(memory_space=pl.ANY), vmem, vmem, vmem, vmem, vmem],
-        out_specs=(vmem, vmem, vmem),
+        in_specs=[vmem, pl.BlockSpec(memory_space=pl.ANY), vmem, vmem, vmem, vmem, vmem, vmem],
+        out_specs=(vmem, vmem, vmem, vmem),
         scratch_shapes=[
             pltpu.VMEM((FEAT, QC), BF16),
+            pltpu.VMEM((32, FEAT), BF16),
             pltpu.VMEM((2, 32, HALF), BF16),
             pltpu.VMEM((32, HALF), BF16),
             pltpu.VMEM((4, CHIP_TOK, ZF), BF16),
@@ -434,32 +581,45 @@
             pltpu.VMEM((TOK, 32), BF16),
             pltpu.VMEM((NCH, TOK, FC), BF16),
             pltpu.VMEM((NCH, TOK, FC), BF16),
-            pltpu.VMEM((NCH, TOK, FC), BF16),
-            pltpu.VMEM((CHIPS - 1, NCH, CHIP_TOK, FC), BF16),
+            pltpu.VMEM((NCH, 4, 2, CHIP_TOK, FC), BF16),
+            pltpu.VMEM((4, 3, 2, CHIP_TOK, FC), BF16),
+            pltpu.VMEM((4, CHIP_TOK, FC), BF16),
+            pltpu.VMEM((4, CHIP_TOK, FC), BF16),
+            pltpu.VMEM((2, 4, CHIP_TOK, FC), BF16),
+            pltpu.VMEM((2, 3, CHIP_TOK, FC), BF16),
             pltpu.VMEM((NCH, 32, FC), BF16),
             pltpu.VMEM((2, NCH, 32, FC), BF16),
             pltpu.VMEM((GC, ZF), F32),
-            pltpu.VMEM((GC, YW), F32),
-            pltpu.VMEM((GC, YW), BF16),
-            pltpu.VMEM((GC, YW), BF16),
-            dma,
+            pltpu.VMEM((BLOCK, QC), F32),
+            pltpu.VMEM((32, YW), F32),
+            pltpu.VMEM((BLOCK, QC), BF16),
+            pltpu.VMEM((BLOCK, QC), BF16),
+            pltpu.VMEM((32, YW), BF16),
+            pltpu.VMEM((32, YW), BF16),
+            dma((2 * NCH,)),
             dma((2,)),
             dma((4,)), dma((4,)),
-            dma((7,)), dma((7,)),
+            dma((4,)), dma((4,)),
+            dma((4, 3)), dma((4, 3)),
+            dma((4, 3)), dma((4, 3)),
             dma((8,)), dma((8,)),
             dma((15,)), dma((15,)),
             dma((7,)), dma((7,)),
             dma((4,)), dma((4,)), dma((4,)), dma((4,)),
             dma((NCH,)), dma((NCH,)),
-            dma((7, NCH)), dma((7, NCH)),
+            dma((4, 3)), dma((4, 3)), dma((4,)), dma((4,)),
+            dma((2,)), dma((2,)), dma((2, 3)), dma((2, 3)),
             dma((NCH,)), dma((NCH,)),
-            dma((2,)),
+            dma((3,)), dma((3,)),
         ],
         compiler_params=pltpu.CompilerParams(
             collective_id=0, has_side_effects=True, vmem_limit_bytes=60 * 1024 * 1024
         ),
-    )(normed, w_query, wkv, query, key, value, grad_context)
-    return grad_input, grad_wq, jnp.transpose(grad_wkv[0:16]), jnp.transpose(grad_wkv[16:32])
+    )(
+        normed, w_query, jnp.transpose(w_key), jnp.transpose(w_value),
+        query, key, value, grad_context,
+    )
+    return grad_input, grad_wq, jnp.transpose(grad_wk), jnp.transpose(grad_wv)
 
 
 def solution(mesh):

time: 139 us -> 102 us (0.73)
  the two profiles are of different devices: /device:TPU:77 before, /device:TPU:95 now
where the time goes in v3:
time: 102 us; the launch traced here: 101 us
  Pallas kernels  94.3 us (92%)
  local copies, waits for them, and re-layouts  6.39 us (6%)
    pallas_call x1, Pallas kernels, shards(): pl.pallas_call(kernel, out_shape=(jax.ShapeDtypeStruct((24, FEAT), BF16),...  94.3 us
    unnamed x4, local copies, waits for them, and re-layouts  6.39 us

profile of v3, /device:TPU:95, one launch (start us, length us, event | category | flops | bytes accessed | tf_op | source)
XLA Modules:
  0.0 101.3 jit_solution(11955952305625286436)
XLA Ops:
  0.6 94.3 %shard_map.111 = (bf16[24,9216]{1,0:T(8,128)(2,1)}, bf16[576,512]{1,0:T(8,128)(2,1)}, bf16[16,576]{1,0:T(8,128)(2,1)}, bf16[16,576]{1,0:T(8,128)(2,1)}) custom-call(bf16[24,9216]{1,0:T(8,128)(2,1)} %normed.1, bf16[9216,512]{1,0:T(8,128)(2,1)} %wq_hbm.1, bf16[16,9216]{1,0:T(8,128)(2,1)} %bitcast.4, bf16[16,9216]{1,0:T(8,128)(2,1)} %bitcast.5, ...), custom_call_target="tpu_custom_call" | custom-call | tf_op jit(solution)/shard_map/pallas_call | solution.py:559
  94.9 1.8 %copy.16 = bf16[24,9216]{1,0:T(8,128)(2,1)} copy(bf16[24,9216]{1,0:T(8,128)(2,1)} %get-tuple-element.16) | data formatting | bytes 884736
  96.7 1.9 %copy.17 = bf16[576,512]{1,0:T(8,128)(2,1)} copy(bf16[576,512]{1,0:T(8,128)(2,1)} %get-tuple-element.17) | data formatting | bytes 1179648
  98.6 1.3 %copy.18 = bf16[576,16]{0,1:T(8,128)(2,1)} copy(bf16[576,16]{0,1:T(8,128)(2,1)} %bitcast.7) | data formatting | bytes 36864
  100.0 1.3 %copy.19 = bf16[576,16]{0,1:T(8,128)(2,1)} copy(bf16[576,16]{0,1:T(8,128)(2,1)} %bitcast.6) | data formatting | bytes 36864

commit v4 on v3

--- a/solution.py
+++ b/solution.py
@@ -99,6 +99,51 @@
     pl.semaphore_wait(barrier, 2 * (NZ - 1) + 1 + 2 * CHIPS - 1)
     s_copy = remote(s_buf.at[other], s_recv, s_sems.at[0], s_sems.at[1], sibling)
     s_copy.start()
+
+    right = (base + lax.rem(z + 1, NZ), mp)
+    left = (base + lax.rem(z + NZ - 1, NZ), mp)
+
+    def ring_pair(h, s, slot_r, slot_l):
+        first = HEAD_DIM * h
+        if s < 4:
+            src_r = gt_buf.at[slot_r, first : first + 256, :]
+            src_l = gt_buf.at[slot_l, first : first + 256, :]
+        else:
+            src_r = gt_buf.at[slot_r, first : first + 128, :]
+            src_l = gt_buf.at[slot_l, first + 128 : first + 256, :]
+        return (
+            remote(src_r, src_r, cw_ss.at[h, s - 1], cw_rs.at[h, s - 1], right),
+            remote(src_l, src_l, cc_ss.at[h, s - 1], cc_rs.at[h, s - 1], left),
+        )
+
+    def ring(h, s):
+        return ring_pair(h, s, lax.rem(z - (s - 1) + NZ, NZ), lax.rem(z + (s - 1), NZ))
+
+    def ring_start(h, s):
+        for copy in ring(h, s):
+            copy.start()
+
+    def ring_wait(h, s):
+        for copy in ring_pair(h, s, lax.rem(z - s + NZ, NZ), lax.rem(z + s, NZ)):
+            copy.wait_recv()
+
+    def kz_pair(s, slot_r, slot_l):
+        src_r, src_l = kv_all.at[slot_r], kv_all.at[slot_l]
+        copies = [remote(src_r, src_r, kz_ss.at[0, s - 1], kz_rs.at[0, s - 1], right)]
+        if s < 4:
+            copies.append(remote(src_l, src_l, kz_ss.at[1, s - 1], kz_rs.at[1, s - 1], left))
+        return copies
+
+    def kz(s):
+        return kz_pair(s, lax.rem(z - (s - 1) + NZ, NZ), lax.rem(z + (s - 1), NZ))
+
+    def kz_start(s):
+        for copy in kz(s):
+            copy.start()
+
+    def kz_wait(s):
+        for copy in kz_pair(s, lax.rem(z - s + NZ, NZ), lax.rem(z + s, NZ)):
+            copy.wait_recv()
 
     key_v = key[...]
     value_v = value[...]
@@ -126,6 +171,7 @@
         gq = dot(key_t, dscore) * scale
         gt_buf[z, HEAD_DIM * h : HEAD_DIM * h + HEAD_DIM, :] = gq.astype(BF16)
         g_buf[:, HEAD_DIM * h : HEAD_DIM * h + HEAD_DIM] = jnp.transpose(gq).astype(BF16)
+        ring_start(h, 1)
         if h == 0:
             s_copy.wait_recv()
             mine = s_buf[core].astype(F32)[:24]
@@ -167,41 +213,6 @@
                 def _(j=j):
                     n_buf[z, chip_rows, :] = t_buf[j]
 
-    right = (base + lax.rem(z + 1, NZ), mp)
-    left = (base + lax.rem(z + NZ - 1, NZ), mp)
-
-    def ring(s):
-        slot_r = lax.rem(z - (s - 1) + NZ, NZ)
-        slot_l = lax.rem(z + (s - 1), NZ)
-        if s < 4:
-            src_r, src_l = gt_buf.at[slot_r], gt_buf.at[slot_l]
-        else:
-            src_r, src_l = gt_buf.at[slot_r, 0:256, :], gt_buf.at[slot_l, 256:512, :]
-        return (
-            remote(src_r, src_r, cw_ss.at[s - 1], cw_rs.at[s - 1], right),
-            remote(src_l, src_l, cc_ss.at[s - 1], cc_rs.at[s - 1], left),
-        )
-
-    def ring_in(s):
-        slot_r = lax.rem(z - s + NZ, NZ)
-        slot_l = lax.rem(z + s, NZ)
-        if s < 4:
-            dst_r, dst_l = gt_buf.at[slot_r], gt_buf.at[slot_l]
-        else:
-            dst_r, dst_l = gt_buf.at[slot_r, 0:256, :], gt_buf.at[slot_l, 256:512, :]
-        return (
-            remote(dst_r, dst_r, cw_ss.at[s - 1], cw_rs.at[s - 1], right),
-            remote(dst_l, dst_l, cc_ss.at[s - 1], cc_rs.at[s - 1], left),
-        )
-
-    def ring_start(s):
-        for copy in ring(s):
-            copy.start()
-
-    def ring_wait(s):
-        for copy in ring_in(s):
-            copy.wait_recv()
-
     kp_t = jnp.transpose(kp * scale)
     vp_t = jnp.transpose(vp)
     kv_buf[:, 0:16, :] = kp_t.reshape(16, 16, TOK).astype(BF16)
@@ -215,7 +226,6 @@
 
     for i in range(1, 2 * CHIPS):
         kv_copy(i).start()
-    ring_start(1)
 
     def n_rows(k):
         return pl.ds(pl.multiple_of(k * CHIP_TOK, 16), CHIP_TOK)
@@ -247,24 +257,13 @@
             k, device = x_from(d), (dp, y_chip * 2 + core)
         return remote(piece(n, k), piece(n, k), agd_ss.at[n, d - 1], agd_rs.at[n, d - 1], device)
 
-    def n_block(half, k):
-        return n_buf.at[pl.ds(4 * half, 4), n_rows(k), :]
-
-    def sib_chip(i):
-        if i == 0:
-            return chip
-        if i == 1:
-            return y_chip
-        k = x_from((i - 2) % 3 + 1)
-        return k if i < 5 else k + 1 - 2 * y_lo
-
-    def sib(i):
-        block = n_block(core, sib_chip(i))
-        return remote(block, block, sib_ss.at[i], sib_rs.at[i], sibling)
-
-    def sib_in(i):
-        block = n_block(other, sib_chip(i))
-        return remote(block, block, sib_ss.at[i], sib_rs.at[i], sibling)
+    def sib(n):
+        block = n_buf.at[4 * core + lax.rem(z + n, 4)]
+        return remote(block, block, sib_ss.at[n], sib_rs.at[n], sibling)
+
+    def sib_in(n):
+        block = n_buf.at[4 * other + lax.rem(z + n, 4)]
+        return remote(block, block, sib_ss.at[n], sib_rs.at[n], sibling)
 
     def ag_first(n):
         j = lax.rem(z + n, 4)
@@ -287,19 +286,17 @@
                 ag_x(n, d).wait_recv()
                 ag_d(n, d).start()
 
-    def ag_last():
-        for n in (1, 3):
+    def ag_last(n):
+        if n % 2 == 0:
+            for d in (1, 3, 2):
+                ag_x(n, d).wait_recv()
+        else:
             ag_y(n).wait_recv()
-        sib(1).start()
         for d in (1, 3, 2):
-            for n in (0, 2):
-                ag_x(n, d).wait_recv()
-            sib(1 + d).start()
-        for d in (1, 3, 2):
-            for n in range(4):
-                ag_d(n, d).wait_recv()
-            sib(4 + d).start()
-
+            ag_d(n, d).wait_recv()
+        sib(n).start()
+
+    ag_first(2)
     for i in range(1, 2 * CHIPS):
         kv_copy(i).wait_recv()
     kv_sum = kv_buf[mp].astype(F32)
@@ -308,21 +305,7 @@
     kv_all[z] = kv_sum.astype(BF16)
     kvg_buf[...] = jnp.transpose(kv_sum).astype(BF16)
 
-    def kz(i):
-        return remote(
-            kv_all.at[z], kv_all.at[z], kz_ss.at[i - 1], kz_rs.at[i - 1],
-            (base + lax.rem(z + i, NZ), mp),
-        )
-
-    def kz_in(i):
-        slot = lax.rem(z - i + NZ, NZ)
-        return remote(
-            kv_all.at[slot], kv_all.at[slot], kz_ss.at[i - 1], kz_rs.at[i - 1],
-            (base + lax.rem(z + i, NZ), mp),
-        )
-
-    for i in range(1, NZ):
-        kz(i).start()
+    kz_start(1)
 
     def partial(half, j):
         first = pl.multiple_of((half * NCH + j) * FC, FC)
@@ -428,8 +411,8 @@
             if with_kv:
                 acc[QC:GC, cols] += dot(low, rhs)
 
-    def wgrad_pair(s):
-        wgrad(lax.rem(z + NZ - s, NZ), lax.rem(z + s, NZ), slice(0, QC), True)
+    def wgrad_pair(n):
+        wgrad(lax.rem(z + n, NZ), lax.rem(z + n + 4, NZ), slice(0, QC), True)
 
     def y_copy(r):
         cols = slice(256 * r, 256 * r + 256)
@@ -446,47 +429,61 @@
 
     acc[...] = jnp.zeros_like(acc)
     sib_half(0)
-    ag_first(0)
+    ag_first(1)
     sib_half(1)
     sib_half(2)
-    ag_first(1)
+    ag_first(3)
     sib_half(3)
-    ag_first(2)
+    ring_wait(0, 1)
+    ring_start(0, 2)
     sib_half(4)
+    ag_first(0)
     sib_half(5)
-    ag_first(3)
-    sib(0).start()
-    ag_second(0)
-    ring_wait(1)
-    ring_start(2)
+    ag_second(2)
+    ring_wait(1, 1)
+    ring_start(1, 2)
+    kz_wait(1)
+    kz_start(2)
     ag_second(1)
     own_half(0)
     own_half(1)
-    ag_second(2)
     ag_second(3)
+    ring_wait(0, 2)
+    ring_start(0, 3)
     own_half(2)
-    ring_wait(2)
-    ring_start(3)
+    ag_second(0)
+    ring_wait(1, 2)
+    ring_start(1, 3)
+    kz_wait(2)
+    kz_start(3)
     own_half(3)
+    ag_last(2)
     own_half(4)
     own_half(5)
+    ag_last(1)
+    ring_wait(0, 3)
+    ring_start(0, 4)
+    sib_in(2).wait_recv()
+    wgrad_pair(2)
+    ring_wait(1, 3)
+    ring_start(1, 4)
+    kz_wait(3)
+    kz_start(4)
     rs_second(0)
-    ag_last()
-    ring_wait(3)
-    ring_start(4)
-    for i in range(1, NZ):
-        kz_in(i).wait_recv()
-    for i in range(CHIPS):
-        sib_in(i).wait_recv()
+    sib_in(1).wait_recv()
     wgrad_pair(1)
+    ag_last(3)
     rs_second(1)
-    wgrad_pair(2)
+    ag_last(0)
     rs_second(2)
+    sib_in(3).wait_recv()
+    wgrad_pair(3)
     rs_second(3)
-    wgrad_pair(3)
-    ring_wait(4)
+    sib_in(0).wait_recv()
+    kz_wait(4)
     for r in range(2):
         rows = slice(256 * r, 256 * r + 256)
+        ring_wait(r, 4)
         wgrad(z, lax.rem(z + 4, NZ), rows, r == 1)
         for q in range(2):
             quarter = slice(256 * r + 128 * q, 256 * r + 128 * q + 128)
@@ -525,17 +522,15 @@
             a2a(j).wait_send()
     for i in range(1, 2 * CHIPS):
         kv_copy(i).wait_send()
-    for i in range(1, NZ):
-        kz(i).wait_send()
     for n in range(4):
         ag_y(n).wait_send()
         for d in range(1, 4):
             ag_x(n, d).wait_send()
             ag_d(n, d).wait_send()
-    for i in range(CHIPS):
-        sib(i).wait_send()
+    for n in range(4):
+        sib(n).wait_send()
     for s in range(1, 5):
-        for copy in ring(s):
+        for copy in (*ring(0, s), *ring(1, s), *kz(s)):
             copy.wait_send()
     for j in range(NCH):
         p_copy(j).wait_send()
@@ -553,18 +548,29 @@
     ykv_copy().wait_send()
 
 
+def place(*refs):
+    sems = refs[-1]
+    copies = [pltpu.make_async_copy(refs[i], refs[4 + i], sems.at[i]) for i in range(4)]
+    for copy in copies:
+        copy.start()
+    for copy in copies:
+        copy.wait()
+
+
 def shards(normed, w_query, w_key, w_value, query, key, value, grad_context):
     vmem = pl.BlockSpec(memory_space=pltpu.VMEM)
     dma = pltpu.SemaphoreType.DMA
-    grad_input, grad_wq, grad_wk, grad_wv = pl.pallas_call(
+    anywhere = pl.BlockSpec(memory_space=pl.ANY)
+    results = (
+        jax.ShapeDtypeStruct((24, FEAT), BF16),
+        jax.ShapeDtypeStruct((BLOCK, QC), BF16),
+        jax.ShapeDtypeStruct((16, BLOCK), BF16),
+        jax.ShapeDtypeStruct((16, BLOCK), BF16),
+    )
+    grads = pl.pallas_call(
         kernel,
-        out_shape=(
-            jax.ShapeDtypeStruct((24, FEAT), BF16),
-            jax.ShapeDtypeStruct((BLOCK, QC), BF16),
-            jax.ShapeDtypeStruct((16, BLOCK), BF16),
-            jax.ShapeDtypeStruct((16, BLOCK), BF16),
-        ),
-        in_specs=[vmem, pl.BlockSpec(memory_space=pl.ANY), vmem, vmem, vmem, vmem, vmem, vmem],
+        out_shape=results,
+        in_specs=[vmem, anywhere, vmem, vmem, vmem, vmem, vmem, vmem],
         out_specs=(vmem, vmem, vmem, vmem),
         scratch_shapes=[
             pltpu.VMEM((FEAT, QC), BF16),
@@ -602,10 +608,10 @@
             dma((4,)), dma((4,)),
             dma((4, 3)), dma((4, 3)),
             dma((4, 3)), dma((4, 3)),
-            dma((8,)), dma((8,)),
+            dma((4,)), dma((4,)),
             dma((15,)), dma((15,)),
-            dma((7,)), dma((7,)),
-            dma((4,)), dma((4,)), dma((4,)), dma((4,)),
+            dma((2, 4)), dma((2, 4)),
+            dma((2, 4)), dma((2, 4)), dma((2, 4)), dma((2, 4)),
             dma((NCH,)), dma((NCH,)),
             dma((4, 3)), dma((4, 3)), dma((4,)), dma((4,)),
             dma((2,)), dma((2,)), dma((2, 3)), dma((2, 3)),
@@ -619,6 +625,14 @@
         normed, w_query, jnp.transpose(w_key), jnp.transpose(w_value),
         query, key, value, grad_context,
     )
+    grad_input, grad_wq, grad_wk, grad_wv = pl.pallas_call(
+        place,
+        out_shape=results,
+        in_specs=[anywhere] * 4,
+        out_specs=(anywhere,) * 4,
+        scratch_shapes=[dma((4,))],
+        compiler_params=pltpu.CompilerParams(vmem_limit_bytes=60 * 1024 * 1024),
+    )(*grads)
     return grad_input, grad_wq, jnp.transpose(grad_wk), jnp.transpose(grad_wv)
 
 

time: 102 us -> 133 us (1.30)
  the two profiles are of different devices: /device:TPU:95 before, /device:TPU:1 now
where the time goes in v4:
time: 133 us
  Pallas kernels  132 us (99%)
    pallas_call x1, Pallas kernels, shards(): pl.pallas_call(kernel, out_shape=results, in_specs=[vmem, anywhere, vmem,...  98.6 us
    pallas_call x1, Pallas kernels, shards(): pl.pallas_call(place, out_shape=results, in_specs=[anywhere] * 4, out_spe...  33.6 us

profile of v4, /device:TPU:1, one launch (start us, length us, event | category | flops | bytes accessed | tf_op | source)
XLA Modules:
  0.0 133.1 jit_solution(13682835903229354281)
XLA Ops:
  0.6 98.6 %shard_map.111 = (bf16[24,9216]{1,0:T(8,128)(2,1)}, bf16[576,512]{1,0:T(8,128)(2,1)}, bf16[16,576]{1,0:T(8,128)(2,1)}, bf16[16,576]{1,0:T(8,128)(2,1)}) custom-call(bf16[24,9216]{1,0:T(8,128)(2,1)} %normed.1, bf16[9216,512]{1,0:T(8,128)(2,1)} %wq_hbm.1, bf16[16,9216]{1,0:T(8,128)(2,1)} %bitcast.4, bf16[16,9216]{1,0:T(8,128)(2,1)} %bitcast.5, ...), custom_call_target="tpu_custom_call" | custom-call | tf_op jit(solution)/shard_map/pallas_call | solution.py:570
  99.3 33.6 %shard_map.112 = (bf16[24,9216]{1,0:T(8,128)(2,1)}, bf16[576,512]{1,0:T(8,128)(2,1)}, bf16[16,576]{1,0:T(8,128)(2,1)}, bf16[16,576]{1,0:T(8,128)(2,1)}) custom-call(bf16[24,9216]{1,0:T(8,128)(2,1)} %get-tuple-element.12.refs_0_, bf16[576,512]{1,0:T(8,128)(2,1)} %get-tuple-element.13.refs_1_, bf16[16,576]{1,0:T(8,128)(2,1)} %get-tuple-element.14.refs_2_, ...), custom_call_target="tpu_custom_call" | custom-call | tf_op jit(solution)/shard_map/pallas_call | solution.py:628

commit v5 on v4

--- a/solution.py
+++ b/solution.py
@@ -171,7 +171,6 @@
         gq = dot(key_t, dscore) * scale
         gt_buf[z, HEAD_DIM * h : HEAD_DIM * h + HEAD_DIM, :] = gq.astype(BF16)
         g_buf[:, HEAD_DIM * h : HEAD_DIM * h + HEAD_DIM] = jnp.transpose(gq).astype(BF16)
-        ring_start(h, 1)
         if h == 0:
             s_copy.wait_recv()
             mine = s_buf[core].astype(F32)[:24]
@@ -230,8 +229,12 @@
     def n_rows(k):
         return pl.ds(pl.multiple_of(k * CHIP_TOK, 16), CHIP_TOK)
 
-    def piece(n, k):
-        return n_buf.at[4 * core + lax.rem(z + n, 4), n_rows(k), :]
+    def piece_z(o):
+        n = jnp.where(core == zhalf, (0, 2, 1, 3)[o], (2, 1, 3, 0)[o])
+        return lax.rem(z + n, 4)
+
+    def piece(o, k):
+        return n_buf.at[4 * core + piece_z(o), n_rows(k), :]
 
     def x_chip(d):
         return lax.rem(x + d, 4) * 2 + y_lo
@@ -258,15 +261,16 @@
         return remote(piece(n, k), piece(n, k), agd_ss.at[n, d - 1], agd_rs.at[n, d - 1], device)
 
     def sib(n):
-        block = n_buf.at[4 * core + lax.rem(z + n, 4)]
+        block = n_buf.at[4 * core + piece_z(n)]
         return remote(block, block, sib_ss.at[n], sib_rs.at[n], sibling)
 
     def sib_in(n):
+        o = jnp.where(core == zhalf, (3, 1, 0, 2)[n], (0, 2, 1, 3)[n])
         block = n_buf.at[4 * other + lax.rem(z + n, 4)]
-        return remote(block, block, sib_ss.at[n], sib_rs.at[n], sibling)
+        return remote(block, block, sib_ss.at[o], sib_rs.at[o], sibling)
 
     def ag_first(n):
-        j = lax.rem(z + n, 4)
+        j = piece_z(n)
 
         @pl.when(4 * core + j != z)
         def _():
@@ -296,7 +300,7 @@
             ag_d(n, d).wait_recv()
         sib(n).start()
 
-    ag_first(2)
+    ag_first(0)
     for i in range(1, 2 * CHIPS):
         kv_copy(i).wait_recv()
     kv_sum = kv_buf[mp].astype(F32)
@@ -304,8 +308,6 @@
         kv_sum = kv_sum + kv_recv[i].astype(F32)
     kv_all[z] = kv_sum.astype(BF16)
     kvg_buf[...] = jnp.transpose(kv_sum).astype(BF16)
-
-    kz_start(1)
 
     def partial(half, j):
         first = pl.multiple_of((half * NCH + j) * FC, FC)
@@ -429,52 +431,55 @@
 
     acc[...] = jnp.zeros_like(acc)
     sib_half(0)
+    sib_half(1)
     ag_first(1)
-    sib_half(1)
+    ring_start(0, 1)
+    ag_first(2)
     sib_half(2)
     ag_first(3)
+    ring_start(1, 1)
+    kz_start(1)
     sib_half(3)
+    sib_half(4)
+    sib_half(5)
+    ag_second(0)
+    ag_second(1)
     ring_wait(0, 1)
     ring_start(0, 2)
-    sib_half(4)
-    ag_first(0)
-    sib_half(5)
+    own_half(0)
+    own_half(1)
     ag_second(2)
     ring_wait(1, 1)
     ring_start(1, 2)
     kz_wait(1)
     kz_start(2)
-    ag_second(1)
-    own_half(0)
-    own_half(1)
     ag_second(3)
+    own_half(2)
     ring_wait(0, 2)
     ring_start(0, 3)
-    own_half(2)
-    ag_second(0)
+    own_half(3)
+    own_half(4)
     ring_wait(1, 2)
     ring_start(1, 3)
     kz_wait(2)
     kz_start(3)
-    own_half(3)
-    ag_last(2)
-    own_half(4)
     own_half(5)
+    ag_last(0)
     ag_last(1)
     ring_wait(0, 3)
     ring_start(0, 4)
-    sib_in(2).wait_recv()
-    wgrad_pair(2)
+    rs_second(0)
+    ag_last(2)
     ring_wait(1, 3)
     ring_start(1, 4)
     kz_wait(3)
     kz_start(4)
-    rs_second(0)
+    ag_last(3)
+    rs_second(1)
+    sib_in(2).wait_recv()
+    wgrad_pair(2)
     sib_in(1).wait_recv()
     wgrad_pair(1)
-    ag_last(3)
-    rs_second(1)
-    ag_last(0)
     rs_second(2)
     sib_in(3).wait_recv()
     wgrad_pair(3)
@@ -549,12 +554,8 @@
 
 
 def place(*refs):
-    sems = refs[-1]
-    copies = [pltpu.make_async_copy(refs[i], refs[4 + i], sems.at[i]) for i in range(4)]
-    for copy in copies:
-        copy.start()
-    for copy in copies:
-        copy.wait()
+    for i in range(4):
+        refs[4 + i][...] = refs[i][...]
 
 
 def shards(normed, w_query, w_key, w_value, query, key, value, grad_context):
@@ -628,10 +629,8 @@
     grad_input, grad_wq, grad_wk, grad_wv = pl.pallas_call(
         place,
         out_shape=results,
-        in_specs=[anywhere] * 4,
-        out_specs=(anywhere,) * 4,
-        scratch_shapes=[dma((4,))],
-        compiler_params=pltpu.CompilerParams(vmem_limit_bytes=60 * 1024 * 1024),
+        in_specs=[vmem] * 4,
+        out_specs=(vmem,) * 4,
     )(*grads)
     return grad_input, grad_wq, jnp.transpose(grad_wk), jnp.transpose(grad_wv)
 

time: 133 us -> 91.6 us (0.69)
  Pallas kernels: 132 us -> 90.8 us
    pallas_call x1, Pallas kernels: 33.6 us -> 2.2 us  [shards(): pl.pallas_call(place, out_shape=results, in_specs=[vmem] * 4, out_specs=(...]
    pallas_call x1, Pallas kernels: 98.6 us -> 88.6 us  [shards(): pl.pallas_call(kernel, out_shape=results, in_specs=[vmem, anywhere, vmem,...]
where the time goes in v5:
time: 91.6 us; the launch traced here: 91.4 us
  Pallas kernels  90.8 us (99%)
    pallas_call x1, Pallas kernels, shards(): pl.pallas_call(kernel, out_shape=results, in_specs=[vmem, anywhere, vmem,...  88.6 us
    pallas_call x1, Pallas kernels, shards(): pl.pallas_call(place, out_shape=results, in_specs=[vmem] * 4, out_specs=(...  2.2 us

profile of v5, /device:TPU:1, one launch (start us, length us, event | category | flops | bytes accessed | tf_op | source)
XLA Modules:
  0.0 91.4 jit_solution(11333604374054854146)
XLA Ops:
  0.6 88.6 %shard_map.111 = (bf16[24,9216]{1,0:T(8,128)(2,1)}, bf16[576,512]{1,0:T(8,128)(2,1)}, bf16[16,576]{1,0:T(8,128)(2,1)}, bf16[16,576]{1,0:T(8,128)(2,1)}) custom-call(bf16[24,9216]{1,0:T(8,128)(2,1)} %normed.1, bf16[9216,512]{1,0:T(8,128)(2,1)} %wq_hbm.1, bf16[16,9216]{1,0:T(8,128)(2,1)} %bitcast.4, bf16[16,9216]{1,0:T(8,128)(2,1)} %bitcast.5, ...), custom_call_target="tpu_custom_call" | custom-call | tf_op jit(solution)/shard_map/pallas_call | solution.py:571
  89.2 2.2 %shard_map.112 = (bf16[24,9216]{1,0:T(8,128)(2,1)}, bf16[576,512]{1,0:T(8,128)(2,1)}, bf16[16,576]{1,0:T(8,128)(2,1)}, bf16[16,576]{1,0:T(8,128)(2,1)}) custom-call(bf16[24,9216]{1,0:T(8,128)(2,1)} %get-tuple-element.12.refs_0_, bf16[576,512]{1,0:T(8,128)(2,1)} %get-tuple-element.13.refs_1_, bf16[16,576]{1,0:T(8,128)(2,1)} %get-tuple-element.14.refs_2_, ...), custom_call_target="tpu_custom_call" | custom-call | tf_op jit(solution)/shard_map/pallas_call | solution.py:629

commit v6 on v5

--- a/solution.py
+++ b/solution.py
@@ -34,12 +34,13 @@
 
 
 def kernel(
-    normed, wq_hbm, wk_t, wv_t, query, key, value, grad,
+    normed_hbm, wq_hbm, wk_hbm, wv_hbm, query_hbm, key_hbm, value_hbm, grad_hbm,
     out_in, out_wq, out_wk, out_wv,
-    w_buf, wkv, s_buf, s_recv, t_buf, n_buf, gt_buf, g_buf, kv_buf, kv_recv, kv_all, kvg_buf,
-    p_send, p_recv, r_buf, rx_recv, rx_send, rx_last, ry_recv, ry_last, f_send, f_buf,
+    normed, wk_t, wv_t, query, key, value, grad,
+    w_buf, wkv, wkv_sib, s_buf, s_recv, t_buf, n_buf, gt_buf, g_buf, kv_buf, kv_sib, kv_recv, kv_all, kvs_recv, kvg_buf,
+    p_send, p_recv, r_buf, rx_mid, rx_recv, rx_send, rx_last, ry_recv, ry_mid, ry_last, f_send, f_buf,
     acc, own_buf, own_kv, y_send, y_recv, ykv_send, ykv_recv,
-    w_sems, s_sems, a2a_ss, a2a_rs, agy_ss, agy_rs, agx_ss, agx_rs, agd_ss, agd_rs,
+    in_sems, w_sems, s_sems, a2a_ss, a2a_rs, agy_ss, agy_rs, agx_ss, agx_rs, agd_ss, agd_rs,
     sib_ss, sib_rs, kv_ss, kv_rs, kz_ss, kz_rs,
     cw_ss, cw_rs, cc_ss, cc_rs, p_ss, p_rs,
     rx_ss, rx_rs, rxy_ss, rxy_rs, ry_ss, ry_rs, ryx_ss, ryx_rs, f_ss, f_rs, y_ss, y_rs,
@@ -71,10 +72,17 @@
             wq_hbm.at[rows, :], w_buf.at[rows, :], w_sems.at[half * NCH + j]
         )
 
-    for j in range(NCH):
-        w_copy(other, j).start()
-    for j in range(NCH):
-        w_copy(core, j).start()
+
+    inputs = (
+        (normed_hbm, normed), (query_hbm, query), (key_hbm, key), (grad_hbm, grad),
+        (value_hbm, value), (wk_hbm, wk_t), (wv_hbm, wv_t),
+    )
+    loads = [
+        pltpu.make_async_copy(there, here, in_sems.at[i])
+        for i, (there, here) in enumerate(inputs)
+    ]
+    for load in loads:
+        load.start()
 
     barrier = pltpu.get_barrier_semaphore()
     for i in range(1, NZ):
@@ -89,8 +97,11 @@
             barrier, inc=1, device_id=(dp, lax.rem(mp + i, 2 * CHIPS)), device_id_type=MESH
         )
 
-    wkv[0:16, :] = wk_t[...]
-    wkv[16:32, :] = wv_t[...]
+    for j in range(NCH):
+        w_copy(other, j).start()
+    for j in range(NCH):
+        w_copy(core, j).start()
+    loads[0].wait()
     for h in range(2):
         for part in range(2):
             cols = normed[:, HALF * part + 2304 * h : HALF * part + 2304 * h + 2304].astype(F32)
@@ -99,6 +110,13 @@
     pl.semaphore_wait(barrier, 2 * (NZ - 1) + 1 + 2 * CHIPS - 1)
     s_copy = remote(s_buf.at[other], s_recv, s_sems.at[0], s_sems.at[1], sibling)
     s_copy.start()
+    loads[5].wait()
+    loads[6].wait()
+    for h in range(2):
+        wkv[h, 0:16, :] = wk_t[:, HALF * h : HALF * h + HALF]
+        wkv[h, 16:32, :] = wv_t[:, HALF * h : HALF * h + HALF]
+    wkv_copy = remote(wkv.at[other], wkv_sib, s_sems.at[2], s_sems.at[3], sibling)
+    wkv_copy.start()
 
     right = (base + lax.rem(z + 1, NZ), mp)
     left = (base + lax.rem(z + NZ - 1, NZ), mp)
@@ -145,6 +163,8 @@
         for copy in kz_pair(s, lax.rem(z - s + NZ, NZ), lax.rem(z + s, NZ)):
             copy.wait_recv()
 
+    for i in range(1, 5):
+        loads[i].wait()
     key_v = key[...]
     value_v = value[...]
     key_t = jnp.transpose(key_v.astype(F32)).astype(BF16)
@@ -214,17 +234,18 @@
 
     kp_t = jnp.transpose(kp * scale)
     vp_t = jnp.transpose(vp)
-    kv_buf[:, 0:16, :] = kp_t.reshape(16, 16, TOK).astype(BF16)
-    kv_buf[:, 16:32, :] = vp_t.reshape(16, 16, TOK).astype(BF16)
+    for c in range(2):
+        kv_buf[c, :, 0:16, :] = kp_t.reshape(CHIPS, 2, 16, TOK)[:, c].astype(BF16)
+        kv_buf[c, :, 16:32, :] = vp_t.reshape(CHIPS, 2, 16, TOK)[:, c].astype(BF16)
+    kv_pair = remote(kv_buf.at[other], kv_sib, kv_ss.at[7], kv_rs.at[7], sibling)
+    kv_pair.start()
 
     def kv_copy(i):
-        there = lax.rem(mp + i, 2 * CHIPS)
+        there = lax.rem(chip + i, CHIPS)
         return remote(
-            kv_buf.at[there], kv_recv.at[i - 1], kv_ss.at[i - 1], kv_rs.at[i - 1], (dp, there)
-        )
-
-    for i in range(1, 2 * CHIPS):
-        kv_copy(i).start()
+            kv_buf.at[core, there], kv_recv.at[i - 1], kv_ss.at[i - 1], kv_rs.at[i - 1],
+            (dp, there * 2 + core),
+        )
 
     def n_rows(k):
         return pl.ds(pl.multiple_of(k * CHIP_TOK, 16), CHIP_TOK)
@@ -248,17 +269,21 @@
         )
 
     def ag_x(n, d):
+        k, to = (x_from(1), 1) if d == 2 else (chip, d)
         return remote(
-            piece(n, chip), piece(n, chip), agx_ss.at[n, d - 1], agx_rs.at[n, d - 1],
-            (dp, x_chip(d) * 2 + core),
+            piece(n, k), piece(n, k), agx_ss.at[n, d - 1], agx_rs.at[n, d - 1],
+            (dp, x_chip(to) * 2 + core),
         )
 
     def ag_d(n, d):
-        if n % 2 == 0:
-            k, device = y_chip, (dp, x_chip(d) * 2 + core)
-        else:
-            k, device = x_from(d), (dp, y_chip * 2 + core)
-        return remote(piece(n, k), piece(n, k), agd_ss.at[n, d - 1], agd_rs.at[n, d - 1], device)
+        if d == 2:
+            k, there = x_from(3) + 1 - 2 * y_lo, x_chip(3)
+        else:
+            k, there = y_chip, x_chip(d)
+        return remote(
+            piece(n, k), piece(n, k), agd_ss.at[n, d - 1], agd_rs.at[n, d - 1],
+            (dp, there * 2 + core),
+        )
 
     def sib(n):
         block = n_buf.at[4 * core + piece_z(n)]
@@ -269,51 +294,47 @@
         block = n_buf.at[4 * other + lax.rem(z + n, 4)]
         return remote(block, block, sib_ss.at[o], sib_rs.at[o], sibling)
 
+    def ag_send(n):
+        ag_y(n).start()
+        ag_x(n, 1).start()
+        ag_x(n, 3).start()
+
     def ag_first(n):
         j = piece_z(n)
-
-        @pl.when(4 * core + j != z)
-        def _():
-            a2a_in(j).wait_recv()
-
-        ag_y(n).start()
-        for d in (1, 3, 2):
-            ag_x(n, d).start()
+        if n == 0:
+            @pl.when(core != zhalf)
+            def _():
+                a2a_in(j).wait_recv()
+                ag_send(0)
+        else:
+            @pl.when(4 * core + j != z)
+            def _():
+                a2a_in(j).wait_recv()
+
+            ag_send(n)
 
     def ag_second(n):
-        if n % 2 == 0:
-            ag_y(n).wait_recv()
-            for d in (1, 3, 2):
-                ag_d(n, d).start()
-        else:
-            for d in (1, 3, 2):
-                ag_x(n, d).wait_recv()
-                ag_d(n, d).start()
+        ag_x(n, 1).wait_recv()
+        ag_x(n, 2).start()
+        ag_y(n).wait_recv()
+        ag_d(n, 1).start()
+        ag_d(n, 3).start()
+
+    def ag_third(n):
+        ag_d(n, 3).wait_recv()
+        ag_d(n, 2).start()
 
     def ag_last(n):
-        if n % 2 == 0:
-            for d in (1, 3, 2):
-                ag_x(n, d).wait_recv()
-        else:
-            ag_y(n).wait_recv()
-        for d in (1, 3, 2):
-            ag_d(n, d).wait_recv()
+        ag_x(n, 3).wait_recv()
+        ag_x(n, 2).wait_recv()
+        ag_d(n, 1).wait_recv()
+        ag_d(n, 2).wait_recv()
         sib(n).start()
-
-    ag_first(0)
-    for i in range(1, 2 * CHIPS):
-        kv_copy(i).wait_recv()
-    kv_sum = kv_buf[mp].astype(F32)
-    for i in range(15):
-        kv_sum = kv_sum + kv_recv[i].astype(F32)
-    kv_all[z] = kv_sum.astype(BF16)
-    kvg_buf[...] = jnp.transpose(kv_sum).astype(BF16)
 
     def partial(half, j):
         first = pl.multiple_of((half * NCH + j) * FC, FC)
         w_copy(half, j).wait()
-        total = dot_nt(g_buf[...], w_buf[pl.ds(first, FC), :])
-        return total + dot(kvg_buf[...], wkv[:, pl.ds(first, FC)])
+        return dot_nt(g_buf[...], w_buf[pl.ds(first, FC), :])
 
     def p_copy(j):
         return remote(p_send.at[j], p_recv.at[j], p_ss.at[j], p_rs.at[j], sibling)
@@ -322,70 +343,106 @@
         p_send[j] = partial(other, j).astype(BF16)
         p_copy(j).start()
 
-    def rx_copy(j, d):
-        n = 2 * (j // 3) + j % 3 - 1
+    def index(j):
+        return j if j < 4 else j - 4
+
+    def x_way(j):
+        return 1 if index(j) % 2 == 0 else 3
+
+    def x_block(j, d):
+        there = lax.rem(x + d, 4)
+        return r_buf.at[j, there] if j >= 4 else r_buf.at[j, there, y_lo]
+
+    def x_copy(j, kind):
+        way = x_way(j)
+        d, to = ((2, way), (way, way), (4 - way, 4 - way))[kind]
+        if j >= 4:
+            n, ss, rs, mid, last = index(j), rx_ss, rx_rs, rx_mid, rx_recv
+        else:
+            n, ss, rs, mid, last = index(j), ryx_ss, ryx_rs, ry_mid, ry_last
+        dst = mid.at[n] if kind == 0 else last.at[n, kind - 1]
         return remote(
-            r_buf.at[j, lax.rem(x + d, 4)], rx_recv.at[n, d - 1],
-            rx_ss.at[n, d - 1], rx_rs.at[n, d - 1], (dp, x_chip(d) * 2 + core),
-        )
+            x_block(j, d), dst, ss.at[n, kind], rs.at[n, kind], (dp, x_chip(to) * 2 + core)
+        )
+
+    def x_first(j):
+        x_copy(j, 0).start()
+        x_copy(j, 2).start()
+
+    def x_mid(j):
+        x_copy(j, 0).wait_recv()
+        there = lax.rem(x + x_way(j), 4)
+        if j >= 4:
+            for k in range(2):
+                r_buf[j, there, k] = (
+                    r_buf[j, there, k].astype(F32) + rx_mid[index(j), k].astype(F32)
+                ).astype(BF16)
+        else:
+            r_buf[j, there, y_lo] = (
+                r_buf[j, there, y_lo].astype(F32) + ry_mid[index(j)].astype(F32)
+            ).astype(BF16)
+        x_copy(j, 1).start()
 
     def rxy_copy(j):
-        n = 2 * (j // 3) + j % 3 - 1
+        n = index(j)
         return remote(
             rx_send.at[n], rx_last.at[n], rxy_ss.at[n], rxy_rs.at[n], (dp, y_chip * 2 + core)
         )
 
     def ry_copy(j):
         return remote(
-            r_buf.at[j, :, 1 - y_lo], ry_recv.at[j // 3], ry_ss.at[j // 3], ry_rs.at[j // 3],
+            r_buf.at[j, :, 1 - y_lo], ry_recv.at[index(j)], ry_ss.at[index(j)], ry_rs.at[index(j)],
             (dp, y_chip * 2 + core),
         )
 
-    def ryx_copy(j, d):
-        return remote(
-            r_buf.at[j, lax.rem(x + d, 4), y_lo], ry_last.at[j // 3, d - 1],
-            ryx_ss.at[j // 3, d - 1], ryx_rs.at[j // 3, d - 1], (dp, x_chip(d) * 2 + core),
-        )
-
     def own_half(j):
-        total = partial(core, j)
+        cols = slice(FC * j, FC * j + FC)
+        both = jnp.concatenate([wkv[core, :, cols], wkv_sib[:, cols]], axis=0)
+        total = partial(core, j) + dot(kvg_buf[...], both)
         p_copy(j).wait_recv()
         total = (total + p_recv[j].astype(F32)).astype(BF16)
         r_buf[j] = total.reshape(4, 2, CHIP_TOK, FC)
-        if j % 3 == 0:
+
+    def own_send(j):
+        if j < 4:
             ry_copy(j).start()
         else:
-            for d in (1, 3, 2):
-                rx_copy(j, d).start()
+            x_first(j)
 
     def rs_second(j):
-        if j % 3 == 0:
+        if j < 4:
             ry_copy(j).wait_recv()
             for k in range(4):
                 r_buf[j, k, y_lo] = (
-                    r_buf[j, k, y_lo].astype(F32) + ry_recv[j // 3, k].astype(F32)
+                    r_buf[j, k, y_lo].astype(F32) + ry_recv[index(j), k].astype(F32)
                 ).astype(BF16)
-            for d in (1, 3, 2):
-                ryx_copy(j, d).start()
-        else:
-            n = 2 * (j // 3) + j % 3 - 1
-            for d in range(1, 4):
-                rx_copy(j, d).wait_recv()
+            x_first(j)
+        else:
+            x_mid(j)
+
+    def rs_third(j):
+        if j < 4:
+            x_mid(j)
+        else:
+            n = index(j)
+            x_copy(j, 1).wait_recv()
+            x_copy(j, 2).wait_recv()
             out = r_buf[j, x, 1 - y_lo].astype(F32)
-            for d in range(3):
+            for d in range(2):
                 out = out + rx_recv[n, d, 1 - y_lo].astype(F32)
             rx_send[n] = out.astype(BF16)
             rxy_copy(j).start()
 
     def rs_last(j):
         total = r_buf[j, x, y_lo].astype(F32)
-        if j % 3 == 0:
-            for d in range(1, 4):
-                ryx_copy(j, d).wait_recv()
-                total = total + ry_last[j // 3, d - 1].astype(F32)
-        else:
-            n = 2 * (j // 3) + j % 3 - 1
-            for d in range(3):
+        if j < 4:
+            x_copy(j, 1).wait_recv()
+            x_copy(j, 2).wait_recv()
+            for d in range(2):
+                total = total + ry_last[index(j), d].astype(F32)
+        else:
+            n = index(j)
+            for d in range(2):
                 total = total + rx_recv[n, d, y_lo].astype(F32)
             rxy_copy(j).wait_recv()
             total = total + rx_last[n].astype(F32)
@@ -430,57 +487,89 @@
         return jnp.where(y_hi == 0, lower, upper), jnp.where(y_hi == 0, upper, lower)
 
     acc[...] = jnp.zeros_like(acc)
+    @pl.when(core == zhalf)
+    def _():
+        ag_send(0)
+
     sib_half(0)
     sib_half(1)
-    ag_first(1)
-    ring_start(0, 1)
-    ag_first(2)
+    kv_pair.wait_recv()
+    kv_buf[core] = (kv_buf[core].astype(F32) + kv_sib[...].astype(F32)).astype(BF16)
+    for i in range(1, CHIPS):
+        kv_copy(i).start()
     sib_half(2)
-    ag_first(3)
-    ring_start(1, 1)
-    kz_start(1)
     sib_half(3)
     sib_half(4)
     sib_half(5)
+    for i in range(1, CHIPS):
+        kv_copy(i).wait_recv()
+    kv_sum = kv_buf[core, chip].astype(F32)
+    for i in range(CHIPS - 1):
+        kv_sum = kv_sum + kv_recv[i].astype(F32)
+    kv_all[z] = kv_sum.astype(BF16)
+    kvs_copy = remote(kv_all.at[z], kvs_recv, s_sems.at[4], s_sems.at[5], sibling)
+    kvs_copy.start()
+    kz_start(1)
+    ag_first(0)
+    ring_start(0, 1)
+    wkv_copy.wait_recv()
+    kvs_copy.wait_recv()
+    kvg_buf[...] = jnp.transpose(
+        jnp.concatenate([kv_sum, kvs_recv[...].astype(F32)], axis=0)
+    ).astype(BF16)
+    own_half(0)
+    ag_first(1)
+    own_half(1)
+    ag_first(2)
+    ring_start(1, 1)
+    own_half(2)
+    ag_first(3)
     ag_second(0)
+    own_half(3)
+    own_send(0)
     ag_second(1)
     ring_wait(0, 1)
     ring_start(0, 2)
-    own_half(0)
-    own_half(1)
+    own_half(4)
+    own_half(5)
     ag_second(2)
+    own_send(1)
+    ag_third(0)
+    ag_second(3)
     ring_wait(1, 1)
     ring_start(1, 2)
     kz_wait(1)
     kz_start(2)
-    ag_second(3)
-    own_half(2)
+    ag_third(1)
+    own_send(2)
+    ag_third(2)
     ring_wait(0, 2)
     ring_start(0, 3)
-    own_half(3)
-    own_half(4)
+    ag_third(3)
+    own_send(3)
+    ag_last(0)
     ring_wait(1, 2)
     ring_start(1, 3)
     kz_wait(2)
     kz_start(3)
-    own_half(5)
-    ag_last(0)
     ag_last(1)
+    rs_second(0)
     ring_wait(0, 3)
     ring_start(0, 4)
-    rs_second(0)
+    sib_in(2).wait_recv()
+    wgrad_pair(2)
+    rs_second(1)
     ag_last(2)
+    own_send(4)
     ring_wait(1, 3)
     ring_start(1, 4)
     kz_wait(3)
     kz_start(4)
-    ag_last(3)
-    rs_second(1)
-    sib_in(2).wait_recv()
-    wgrad_pair(2)
     sib_in(1).wait_recv()
     wgrad_pair(1)
+    own_send(5)
     rs_second(2)
+    ag_last(3)
     sib_in(3).wait_recv()
     wgrad_pair(3)
     rs_second(3)
@@ -500,10 +589,20 @@
     own_kv[...] = mine
     ykv_send[...] = theirs.astype(BF16)
     ykv_copy().start()
+    rs_third(0)
+    rs_third(1)
     rs_second(4)
+    rs_third(2)
     rs_second(5)
-    for j in range(NCH):
-        rs_last(j)
+    rs_third(3)
+    rs_third(4)
+    rs_third(5)
+    rs_last(0)
+    rs_last(1)
+    rs_last(2)
+    rs_last(3)
+    rs_last(4)
+    rs_last(5)
     for j in range(NCH):
         f_in(j).wait_recv()
     for h in range(2):
@@ -525,7 +624,10 @@
         @pl.when(4 * core + j != z)
         def _(j=j):
             a2a(j).wait_send()
-    for i in range(1, 2 * CHIPS):
+    kv_pair.wait_send()
+    wkv_copy.wait_send()
+    kvs_copy.wait_send()
+    for i in range(1, CHIPS):
         kv_copy(i).wait_send()
     for n in range(4):
         ag_y(n).wait_send()
@@ -540,14 +642,12 @@
     for j in range(NCH):
         p_copy(j).wait_send()
         f_copy(j).wait_send()
-        if j % 3 == 0:
+        if j < 4:
             ry_copy(j).wait_send()
-            for d in range(1, 4):
-                ryx_copy(j, d).wait_send()
-        else:
-            for d in range(1, 4):
-                rx_copy(j, d).wait_send()
+        else:
             rxy_copy(j).wait_send()
+        for kind in range(3):
+            x_copy(j, kind).wait_send()
     for r in range(2):
         y_copy(r).wait_send()
     ykv_copy().wait_send()
@@ -571,29 +671,41 @@
     grads = pl.pallas_call(
         kernel,
         out_shape=results,
-        in_specs=[vmem, anywhere, vmem, vmem, vmem, vmem, vmem, vmem],
+        in_specs=[anywhere] * 8,
         out_specs=(vmem, vmem, vmem, vmem),
         scratch_shapes=[
+            pltpu.VMEM((24, FEAT), BF16),
+            pltpu.VMEM((16, FEAT), BF16),
+            pltpu.VMEM((16, FEAT), BF16),
+            pltpu.VMEM((TOK, QC), BF16),
+            pltpu.VMEM((TOK, HEAD_DIM), BF16),
+            pltpu.VMEM((TOK, HEAD_DIM), BF16),
+            pltpu.VMEM((TOK, QC), BF16),
             pltpu.VMEM((FEAT, QC), BF16),
-            pltpu.VMEM((32, FEAT), BF16),
+            pltpu.VMEM((2, 32, HALF), BF16),
+            pltpu.VMEM((32, HALF), BF16),
             pltpu.VMEM((2, 32, HALF), BF16),
             pltpu.VMEM((32, HALF), BF16),
             pltpu.VMEM((4, CHIP_TOK, ZF), BF16),
             pltpu.VMEM((NZ, TOK, ZF), BF16),
             pltpu.VMEM((NZ, QC, TOK), BF16),
             pltpu.VMEM((TOK, QC), BF16),
-            pltpu.VMEM((16, 32, TOK), BF16),
-            pltpu.VMEM((15, 32, TOK), BF16),
+            pltpu.VMEM((2, CHIPS, 32, TOK), BF16),
+            pltpu.VMEM((CHIPS, 32, TOK), BF16),
+            pltpu.VMEM((CHIPS - 1, 32, TOK), BF16),
             pltpu.VMEM((NZ, 32, TOK), BF16),
-            pltpu.VMEM((TOK, 32), BF16),
+            pltpu.VMEM((32, TOK), BF16),
+            pltpu.VMEM((TOK, 64), BF16),
             pltpu.VMEM((NCH, TOK, FC), BF16),
             pltpu.VMEM((NCH, TOK, FC), BF16),
             pltpu.VMEM((NCH, 4, 2, CHIP_TOK, FC), BF16),
-            pltpu.VMEM((4, 3, 2, CHIP_TOK, FC), BF16),
+            pltpu.VMEM((2, 2, CHIP_TOK, FC), BF16),
+            pltpu.VMEM((2, 2, 2, CHIP_TOK, FC), BF16),
+            pltpu.VMEM((2, CHIP_TOK, FC), BF16),
+            pltpu.VMEM((2, CHIP_TOK, FC), BF16),
+            pltpu.VMEM((4, 4, CHIP_TOK, FC), BF16),
             pltpu.VMEM((4, CHIP_TOK, FC), BF16),
-            pltpu.VMEM((4, CHIP_TOK, FC), BF16),
-            pltpu.VMEM((2, 4, CHIP_TOK, FC), BF16),
-            pltpu.VMEM((2, 3, CHIP_TOK, FC), BF16),
+            pltpu.VMEM((4, 2, CHIP_TOK, FC), BF16),
             pltpu.VMEM((NCH, 32, FC), BF16),
             pltpu.VMEM((2, NCH, 32, FC), BF16),
             pltpu.VMEM((GC, ZF), F32),
@@ -603,19 +715,20 @@
             pltpu.VMEM((BLOCK, QC), BF16),
             pltpu.VMEM((32, YW), BF16),
             pltpu.VMEM((32, YW), BF16),
+            dma((7,)),
             dma((2 * NCH,)),
-            dma((2,)),
+            dma((6,)),
             dma((4,)), dma((4,)),
             dma((4,)), dma((4,)),
             dma((4, 3)), dma((4, 3)),
             dma((4, 3)), dma((4, 3)),
             dma((4,)), dma((4,)),
-            dma((15,)), dma((15,)),
+            dma((8,)), dma((8,)),
             dma((2, 4)), dma((2, 4)),
             dma((2, 4)), dma((2, 4)), dma((2, 4)), dma((2, 4)),
             dma((NCH,)), dma((NCH,)),
-            dma((4, 3)), dma((4, 3)), dma((4,)), dma((4,)),
-            dma((2,)), dma((2,)), dma((2, 3)), dma((2, 3)),
+            dma((2, 3)), dma((2, 3)), dma((2,)), dma((2,)),
+            dma((4,)), dma((4,)), dma((4, 3)), dma((4, 3)),
             dma((NCH,)), dma((NCH,)),
             dma((3,)), dma((3,)),
         ],

time: 91.6 us -> 85.3 us (0.931)
  Pallas kernels: 90.8 us -> 84.6 us
    pallas_call x1, Pallas kernels: 88.6 us -> 82.4 us  [shards(): pl.pallas_call(kernel, out_shape=results, in_specs=[anywhere] * 8, out_sp...]
where the time goes in v6:
time: 85.3 us; the launch traced here: 85.2 us
  Pallas kernels  84.6 us (99%)
    pallas_call x1, Pallas kernels, shards(): pl.pallas_call(kernel, out_shape=results, in_specs=[anywhere] * 8, out_sp...  82.4 us
    pallas_call x1, Pallas kernels, shards(): pl.pallas_call(place, out_shape=results, in_specs=[vmem] * 4, out_specs=(...  2.2 us

profile of v6, /device:TPU:1, one launch (start us, length us, event | category | flops | bytes accessed | tf_op | source)
XLA Modules:
  0.0 85.2 jit_solution(12524668950517202327)
XLA Ops:
  0.6 82.4 %shard_map.111 = (bf16[24,9216]{1,0:T(8,128)(2,1)}, bf16[576,512]{1,0:T(8,128)(2,1)}, bf16[16,576]{1,0:T(8,128)(2,1)}, bf16[16,576]{1,0:T(8,128)(2,1)}) custom-call(bf16[24,9216]{1,0:T(8,128)(2,1)} %normed_hbm.1, bf16[9216,512]{1,0:T(8,128)(2,1)} %wq_hbm.1, bf16[16,9216]{1,0:T(8,128)(2,1)} %bitcast.4, bf16[16,9216]{1,0:T(8,128)(2,1)} %bitcast.5, ...), custom_call_target="tpu_custom_call" | custom-call | tf_op jit(solution)/shard_map/pallas_call | solution.py:671
  83.0 2.2 %shard_map.112 = (bf16[24,9216]{1,0:T(8,128)(2,1)}, bf16[576,512]{1,0:T(8,128)(2,1)}, bf16[16,576]{1,0:T(8,128)(2,1)}, bf16[16,576]{1,0:T(8,128)(2,1)}) custom-call(bf16[24,9216]{1,0:T(8,128)(2,1)} %get-tuple-element.12.refs_0_, bf16[576,512]{1,0:T(8,128)(2,1)} %get-tuple-element.13.refs_1_, bf16[16,576]{1,0:T(8,128)(2,1)} %get-tuple-element.14.refs_2_, ...), custom_call_target="tpu_custom_call" | custom-call | tf_op jit(solution)/shard_map/pallas_call | solution.py:742

commit v7 on v6

--- a/solution.py
+++ b/solution.py
@@ -35,12 +35,13 @@
 
 def kernel(
     normed_hbm, wq_hbm, wk_hbm, wv_hbm, query_hbm, key_hbm, value_hbm, grad_hbm,
+    in_hbm, wq_out_hbm, wk_out_hbm, wv_out_hbm,
     out_in, out_wq, out_wk, out_wv,
     normed, wk_t, wv_t, query, key, value, grad,
     w_buf, wkv, wkv_sib, s_buf, s_recv, t_buf, n_buf, gt_buf, g_buf, kv_buf, kv_sib, kv_recv, kv_all, kvs_recv, kvg_buf,
     p_send, p_recv, r_buf, rx_mid, rx_recv, rx_send, rx_last, ry_recv, ry_mid, ry_last, f_send, f_buf,
     acc, own_buf, own_kv, y_send, y_recv, ykv_send, ykv_recv,
-    in_sems, w_sems, s_sems, a2a_ss, a2a_rs, agy_ss, agy_rs, agx_ss, agx_rs, agd_ss, agd_rs,
+    out_sems, in_sems, w_sems, s_sems, a2a_ss, a2a_rs, agy_ss, agy_rs, agx_ss, agx_rs, agd_ss, agd_rs,
     sib_ss, sib_rs, kv_ss, kv_rs, kz_ss, kz_rs,
     cw_ss, cw_rs, cc_ss, cc_rs, p_ss, p_rs,
     rx_ss, rx_rs, rxy_ss, rxy_rs, ry_ss, ry_rs, ryx_ss, ryx_rs, f_ss, f_rs, y_ss, y_rs,
@@ -162,6 +163,12 @@
     def kz_wait(s):
         for copy in kz_pair(s, lax.rem(z - s + NZ, NZ), lax.rem(z + s, NZ)):
             copy.wait_recv()
+
+    def piece_n(o):
+        return jnp.where(core == zhalf, (0, 2, 1, 3)[o], (2, 1, 3, 0)[o])
+
+    def piece_z(o):
+        return lax.rem(z + piece_n(o), 4)
 
     for i in range(1, 5):
         loads[i].wait()
@@ -223,14 +230,19 @@
                     (base + peer, chip * 2 + zhalf),
                 )
 
-            for j in range(4):
+            def a2a_send(o):
+                j = lax.rem(z + 4 - piece_n(o), 4)
+
                 @pl.when(4 * core + j != z)
-                def _(j=j):
+                def _():
                     a2a(j).start()
 
                 @pl.when(4 * core + j == z)
-                def _(j=j):
+                def _():
                     n_buf[z, chip_rows, :] = t_buf[j]
+
+            a2a_send(0)
+            a2a_send(1)
 
     kp_t = jnp.transpose(kp * scale)
     vp_t = jnp.transpose(vp)
@@ -249,10 +261,6 @@
 
     def n_rows(k):
         return pl.ds(pl.multiple_of(k * CHIP_TOK, 16), CHIP_TOK)
-
-    def piece_z(o):
-        n = jnp.where(core == zhalf, (0, 2, 1, 3)[o], (2, 1, 3, 0)[o])
-        return lax.rem(z + n, 4)
 
     def piece(o, k):
         return n_buf.at[4 * core + piece_z(o), n_rows(k), :]
@@ -460,15 +468,15 @@
     def f_in(j):
         return remote(f_send.at[j], f_buf.at[other, j], f_ss.at[j], f_rs.at[j], sibling)
 
-    def wgrad(za, zb, top_rows, with_kv):
-        top = jnp.concatenate([gt_buf[za, top_rows, :], gt_buf[zb, top_rows, :]], axis=1)
-        low = jnp.concatenate([kv_all[za], kv_all[zb]], axis=1)
-        for c in range(3):
-            cols = slice(TOK * c, TOK * c + TOK)
+    def wgrad(za, zb, first, with_kv):
+        lhs = [jnp.concatenate([gt_buf[za, first, :], gt_buf[zb, first, :]], axis=1)]
+        if with_kv:
+            lhs.append(jnp.concatenate([kv_all[za], kv_all[zb]], axis=1))
+        lhs = jnp.concatenate(lhs, axis=0)
+        rows = slice(first.start, first.start + lhs.shape[0])
+        for cols in (slice(0, 512), slice(512, 1024), slice(1024, ZF)):
             rhs = jnp.concatenate([n_buf[za, :, cols], n_buf[zb, :, cols]], axis=0)
-            acc[top_rows, cols] += dot(top, rhs)
-            if with_kv:
-                acc[QC:GC, cols] += dot(low, rhs)
+            acc[rows, cols] += dot(lhs, rhs)
 
     def wgrad_pair(n):
         wgrad(lax.rem(z + n, NZ), lax.rem(z + n + 4, NZ), slice(0, QC), True)
@@ -497,8 +505,10 @@
     kv_buf[core] = (kv_buf[core].astype(F32) + kv_sib[...].astype(F32)).astype(BF16)
     for i in range(1, CHIPS):
         kv_copy(i).start()
+    a2a_send(2)
     sib_half(2)
     sib_half(3)
+    a2a_send(3)
     sib_half(4)
     sib_half(5)
     for i in range(1, CHIPS):
@@ -556,11 +566,11 @@
     rs_second(0)
     ring_wait(0, 3)
     ring_start(0, 4)
+    own_send(4)
     sib_in(2).wait_recv()
     wgrad_pair(2)
     rs_second(1)
     ag_last(2)
-    own_send(4)
     ring_wait(1, 3)
     ring_start(1, 4)
     kz_wait(3)
@@ -573,6 +583,7 @@
     sib_in(3).wait_recv()
     wgrad_pair(3)
     rs_second(3)
+    rs_second(4)
     sib_in(0).wait_recv()
     kz_wait(4)
     for r in range(2):
@@ -591,7 +602,6 @@
     ykv_copy().start()
     rs_third(0)
     rs_third(1)
-    rs_second(4)
     rs_third(2)
     rs_second(5)
     rs_third(3)
@@ -601,24 +611,6 @@
     rs_last(1)
     rs_last(2)
     rs_last(3)
-    rs_last(4)
-    rs_last(5)
-    for j in range(NCH):
-        f_in(j).wait_recv()
-    for h in range(2):
-        for j in range(NCH):
-            out_in[:, HALF * h + FC * j : HALF * h + FC * j + FC] = f_buf[h, j].astype(F32)[
-                0:24
-            ].astype(BF16)
-    for r in range(2):
-        y_copy(r).wait_recv()
-        cols = slice(256 * r, 256 * r + 256)
-        out_wq[:, cols] = (own_buf[:, cols] + y_recv[:, cols].astype(F32)).astype(BF16)
-    ykv_copy().wait_recv()
-    total = (own_kv[...] + ykv_recv[...].astype(F32))[:, 0:BLOCK].astype(BF16)
-    out_wk[...] = total[0:16]
-    out_wv[...] = total[16:32]
-
     s_copy.wait_send()
     for j in range(4):
         @pl.when(4 * core + j != z)
@@ -641,25 +633,67 @@
             copy.wait_send()
     for j in range(NCH):
         p_copy(j).wait_send()
-        f_copy(j).wait_send()
         if j < 4:
             ry_copy(j).wait_send()
-        else:
-            rxy_copy(j).wait_send()
         for kind in range(3):
             x_copy(j, kind).wait_send()
+    rs_last(4)
+    rs_last(5)
+    outs = []
+    for r in range(2):
+        y_copy(r).wait_recv()
+        cols = slice(256 * r, 256 * r + 256)
+        out_wq[:, cols] = (own_buf[:, cols] + y_recv[:, cols].astype(F32)).astype(BF16)
+        outs.append(
+            pltpu.make_async_copy(out_wq.at[:, cols], wq_out_hbm.at[:, cols], out_sems.at[r])
+        )
+        outs[-1].start()
+    ykv_copy().wait_recv()
+    total = (own_kv[...] + ykv_recv[...].astype(F32))[:, 0:BLOCK].astype(BF16)
+    out_wk[...] = total[0:16]
+    out_wv[...] = total[16:32]
+    outs.append(pltpu.make_async_copy(out_wk, wk_out_hbm, out_sems.at[2]))
+    outs[-1].start()
+    outs.append(pltpu.make_async_copy(out_wv, wv_out_hbm, out_sems.at[3]))
+    outs[-1].start()
+    for j in range(NCH):
+        f_in(j).wait_recv()
+    for h in range(2):
+        for j in range(NCH):
+            out_in[:, HALF * h + FC * j : HALF * h + FC * j + FC] = f_buf[h, j].astype(F32)[
+                0:24
+            ].astype(BF16)
+    outs.append(pltpu.make_async_copy(out_in, in_hbm, out_sems.at[4]))
+    outs[-1].start()
+    for j in range(NCH):
+        f_copy(j).wait_send()
+        if j >= 4:
+            rxy_copy(j).wait_send()
     for r in range(2):
         y_copy(r).wait_send()
     ykv_copy().wait_send()
+    for out in outs:
+        out.wait()
 
 
 def place(*refs):
-    for i in range(4):
-        refs[4 + i][...] = refs[i][...]
+    ins, outs, held, sems = refs[0:4], refs[4:8], refs[8:12], refs[12]
+    parts = [(0, slice(0, 24)), (1, slice(0, 288)), (1, slice(288, 576))]
+    parts += [(2, slice(0, 16)), (3, slice(0, 16))]
+    first = []
+    for n, (i, rows) in enumerate(parts):
+        first.append(pltpu.make_async_copy(ins[i].at[rows], held[i].at[rows], sems.at[n, 0]))
+        first[-1].start()
+    second = []
+    for n, (i, rows) in enumerate(parts):
+        first[n].wait()
+        second.append(pltpu.make_async_copy(held[i].at[rows], outs[i].at[rows], sems.at[n, 1]))
+        second[-1].start()
+    for copy in second:
+        copy.wait()
 
 
 def shards(normed, w_query, w_key, w_value, query, key, value, grad_context):
-    vmem = pl.BlockSpec(memory_space=pltpu.VMEM)
     dma = pltpu.SemaphoreType.DMA
     anywhere = pl.BlockSpec(memory_space=pl.ANY)
     results = (
@@ -672,8 +706,12 @@
         kernel,
         out_shape=results,
         in_specs=[anywhere] * 8,
-        out_specs=(vmem, vmem, vmem, vmem),
+        out_specs=(anywhere,) * 4,
         scratch_shapes=[
+            pltpu.VMEM((24, FEAT), BF16),
+            pltpu.VMEM((BLOCK, QC), BF16),
+            pltpu.VMEM((16, BLOCK), BF16),
+            pltpu.VMEM((16, BLOCK), BF16),
             pltpu.VMEM((24, FEAT), BF16),
             pltpu.VMEM((16, FEAT), BF16),
             pltpu.VMEM((16, FEAT), BF16),
@@ -715,6 +753,7 @@
             pltpu.VMEM((BLOCK, QC), BF16),
             pltpu.VMEM((32, YW), BF16),
             pltpu.VMEM((32, YW), BF16),
+            dma((5,)),
             dma((7,)),
             dma((2 * NCH,)),
             dma((6,)),
@@ -742,8 +781,10 @@
     grad_input, grad_wq, grad_wk, grad_wv = pl.pallas_call(
         place,
         out_shape=results,
-        in_specs=[vmem] * 4,
-        out_specs=(vmem,) * 4,
+        in_specs=[anywhere] * 4,
+        out_specs=(anywhere,) * 4,
+        scratch_shapes=[pltpu.VMEM(result.shape, BF16) for result in results] + [dma((5, 2))],
+        compiler_params=pltpu.CompilerParams(vmem_limit_bytes=60 * 1024 * 1024),
     )(*grads)
     return grad_input, grad_wq, jnp.transpose(grad_wk), jnp.transpose(grad_wv)
 

time: 85.3 us -> 83 us (0.973)
  Pallas kernels: 84.6 us -> 82.1 us
    pallas_call x1, Pallas kernels: 82.4 us -> 80 us  [shards(): pl.pallas_call(kernel, out_shape=results, in_specs=[anywhere] * 8, out_sp...]
where the time goes in v7:
time: 83 us; the launch traced here: 82.9 us
  Pallas kernels  82.1 us (99%)
    pallas_call x1, Pallas kernels, shards(): pl.pallas_call(kernel, out_shape=results, in_specs=[anywhere] * 8, out_sp...  80 us
    pallas_call x1, Pallas kernels, shards(): pl.pallas_call(place, out_shape=results, in_specs=[anywhere] * 4, out_spe...  2.06 us

profile of v7, /device:TPU:1, one launch (start us, length us, event | category | flops | bytes accessed | tf_op | source)
XLA Modules:
  0.0 82.9 jit_solution(15134826327261513144)
XLA Ops:
  0.6 80.0 %shard_map.111 = (bf16[24,9216]{1,0:T(8,128)(2,1)}, bf16[576,512]{1,0:T(8,128)(2,1)}, bf16[16,576]{1,0:T(8,128)(2,1)}, bf16[16,576]{1,0:T(8,128)(2,1)}) custom-call(bf16[24,9216]{1,0:T(8,128)(2,1)} %normed_hbm.1, bf16[9216,512]{1,0:T(8,128)(2,1)} %wq_hbm.1, bf16[16,9216]{1,0:T(8,128)(2,1)} %bitcast.4, bf16[16,9216]{1,0:T(8,128)(2,1)} %bitcast.5, ...), custom_call_target="tpu_custom_call" | custom-call | tf_op jit(solution)/shard_map/pallas_call | solution.py:705
  80.6 2.1 %shard_map.112 = (bf16[24,9216]{1,0:T(8,128)(2,1)}, bf16[576,512]{1,0:T(8,128)(2,1)}, bf16[16,576]{1,0:T(8,128)(2,1)}, bf16[16,576]{1,0:T(8,128)(2,1)}) custom-call(bf16[24,9216]{1,0:T(8,128)(2,1)} %get-tuple-element.12.refs_0_, bf16[576,512]{1,0:T(8,128)(2,1)} %get-tuple-element.13.refs_1_, bf16[16,576]{1,0:T(8,128)(2,1)} %get-tuple-element.14.refs_2_, ...), custom_call_target="tpu_custom_call" | custom-call | tf_op jit(solution)/shard_map/pallas_call | solution.py:781

commit v8 on v7

--- a/solution.py
+++ b/solution.py
@@ -34,10 +34,10 @@
 
 
 def kernel(
-    normed_hbm, wq_hbm, wk_hbm, wv_hbm, query_hbm, key_hbm, value_hbm, grad_hbm,
-    in_hbm, wq_out_hbm, wk_out_hbm, wv_out_hbm,
-    out_in, out_wq, out_wk, out_wv,
-    normed, wk_t, wv_t, query, key, value, grad,
+    normed, wq_hbm, wk_hbm, wv_hbm, query_hbm, key_hbm, value_hbm, grad_hbm,
+    out_in, wq_out_hbm, wk_out_hbm, wv_out_hbm,
+    out_wq, out_wk, out_wv,
+    wk_t, wv_t, query, key, value, grad,
     w_buf, wkv, wkv_sib, s_buf, s_recv, t_buf, n_buf, gt_buf, g_buf, kv_buf, kv_sib, kv_recv, kv_all, kvs_recv, kvg_buf,
     p_send, p_recv, r_buf, rx_mid, rx_recv, rx_send, rx_last, ry_recv, ry_mid, ry_last, f_send, f_buf,
     acc, own_buf, own_kv, y_send, y_recv, ykv_send, ykv_recv,
@@ -75,7 +75,7 @@
 
 
     inputs = (
-        (normed_hbm, normed), (query_hbm, query), (key_hbm, key), (grad_hbm, grad),
+        (query_hbm, query), (key_hbm, key), (grad_hbm, grad),
         (value_hbm, value), (wk_hbm, wk_t), (wv_hbm, wv_t),
     )
     loads = [
@@ -102,7 +102,6 @@
         w_copy(other, j).start()
     for j in range(NCH):
         w_copy(core, j).start()
-    loads[0].wait()
     for h in range(2):
         for part in range(2):
             cols = normed[:, HALF * part + 2304 * h : HALF * part + 2304 * h + 2304].astype(F32)
@@ -111,8 +110,8 @@
     pl.semaphore_wait(barrier, 2 * (NZ - 1) + 1 + 2 * CHIPS - 1)
     s_copy = remote(s_buf.at[other], s_recv, s_sems.at[0], s_sems.at[1], sibling)
     s_copy.start()
+    loads[4].wait()
     loads[5].wait()
-    loads[6].wait()
     for h in range(2):
         wkv[h, 0:16, :] = wk_t[:, HALF * h : HALF * h + HALF]
         wkv[h, 16:32, :] = wv_t[:, HALF * h : HALF * h + HALF]
@@ -170,7 +169,7 @@
     def piece_z(o):
         return lax.rem(z + piece_n(o), 4)
 
-    for i in range(1, 5):
+    for i in range(4):
         loads[i].wait()
     key_v = key[...]
     value_v = value[...]
@@ -663,8 +662,6 @@
             out_in[:, HALF * h + FC * j : HALF * h + FC * j + FC] = f_buf[h, j].astype(F32)[
                 0:24
             ].astype(BF16)
-    outs.append(pltpu.make_async_copy(out_in, in_hbm, out_sems.at[4]))
-    outs[-1].start()
     for j in range(NCH):
         f_copy(j).wait_send()
         if j >= 4:
@@ -677,14 +674,15 @@
 
 
 def place(*refs):
-    ins, outs, held, sems = refs[0:4], refs[4:8], refs[8:12], refs[12]
-    parts = [(0, slice(0, 24)), (1, slice(0, 288)), (1, slice(288, 576))]
+    ins, outs, held, sems = refs[0:4], refs[4:8], (None, *refs[8:11]), refs[11]
+    parts = [(1, slice(0, 288)), (1, slice(288, 576))]
     parts += [(2, slice(0, 16)), (3, slice(0, 16))]
     first = []
     for n, (i, rows) in enumerate(parts):
         first.append(pltpu.make_async_copy(ins[i].at[rows], held[i].at[rows], sems.at[n, 0]))
         first[-1].start()
     second = []
+    outs[0][...] = ins[0][...]
     for n, (i, rows) in enumerate(parts):
         first[n].wait()
         second.append(pltpu.make_async_copy(held[i].at[rows], outs[i].at[rows], sems.at[n, 1]))
@@ -695,6 +693,7 @@
 
 def shards(normed, w_query, w_key, w_value, query, key, value, grad_context):
     dma = pltpu.SemaphoreType.DMA
+    vmem = pl.BlockSpec(memory_space=pltpu.VMEM)
     anywhere = pl.BlockSpec(memory_space=pl.ANY)
     results = (
         jax.ShapeDtypeStruct((24, FEAT), BF16),
@@ -705,14 +704,12 @@
     grads = pl.pallas_call(
         kernel,
         out_shape=results,
-        in_specs=[anywhere] * 8,
-        out_specs=(anywhere,) * 4,
+        in_specs=[vmem] + [anywhere] * 7,
+        out_specs=(vmem,) + (anywhere,) * 3,
         scratch_shapes=[
-            pltpu.VMEM((24, FEAT), BF16),
             pltpu.VMEM((BLOCK, QC), BF16),
             pltpu.VMEM((16, BLOCK), BF16),
             pltpu.VMEM((16, BLOCK), BF16),
-            pltpu.VMEM((24, FEAT), BF16),
             pltpu.VMEM((16, FEAT), BF16),
             pltpu.VMEM((16, FEAT), BF16),
             pltpu.VMEM((TOK, QC), BF16),
@@ -753,8 +750,8 @@
             pltpu.VMEM((BLOCK, QC), BF16),
             pltpu.VMEM((32, YW), BF16),
             pltpu.VMEM((32, YW), BF16),
-            dma((5,)),
-            dma((7,)),
+            dma((4,)),
+            dma((6,)),
             dma((2 * NCH,)),
             dma((6,)),
             dma((4,)), dma((4,)),
@@ -781,9 +778,9 @@
     grad_input, grad_wq, grad_wk, grad_wv = pl.pallas_call(
         place,
         out_shape=results,
-        in_specs=[anywhere] * 4,
-        out_specs=(anywhere,) * 4,
-        scratch_shapes=[pltpu.VMEM(result.shape, BF16) for result in results] + [dma((5, 2))],
+        in_specs=[vmem] + [anywhere] * 3,
+        out_specs=(vmem,) + (anywhere,) * 3,
+        scratch_shapes=[pltpu.VMEM(result.shape, BF16) for result in results[1:]] + [dma((4, 2))],
         compiler_params=pltpu.CompilerParams(vmem_limit_bytes=60 * 1024 * 1024),
     )(*grads)
     return grad_input, grad_wq, jnp.transpose(grad_wk), jnp.transpose(grad_wv)

time: 83 us -> 85.5 us (1.030)
  Pallas kernels: 82.1 us -> 84.5 us
    pallas_call x2, Pallas kernels: 82.1 us -> 84.5 us  [the longest x1 80.9 us: shards(): pl.pallas_call(kernel, out_shape=results, in_specs=[vmem] + [anywhere] *...]
where the time goes in v8:
time: 85.5 us; the launch traced here: 85.3 us
  Pallas kernels  84.5 us (99%)
    pallas_call x1, Pallas kernels, shards(): pl.pallas_call(kernel, out_shape=results, in_specs=[vmem] + [anywhere] *...  80.9 us
    pallas_call x1, Pallas kernels, shards(): pl.pallas_call(place, out_shape=results, in_specs=[vmem] + [anywhere] * 3...  3.62 us

profile of v8, /device:TPU:1, one launch (start us, length us, event | category | flops | bytes accessed | tf_op | source)
XLA Modules:
  0.0 85.3 jit_solution(3649060069883306499)
XLA Ops:
  0.6 80.9 %shard_map.111 = (bf16[24,9216]{1,0:T(8,128)(2,1)}, bf16[576,512]{1,0:T(8,128)(2,1)}, bf16[16,576]{1,0:T(8,128)(2,1)}, bf16[16,576]{1,0:T(8,128)(2,1)}) custom-call(bf16[24,9216]{1,0:T(8,128)(2,1)} %normed.1, bf16[9216,512]{1,0:T(8,128)(2,1)} %wq_hbm.1, bf16[16,9216]{1,0:T(8,128)(2,1)} %bitcast.4, bf16[16,9216]{1,0:T(8,128)(2,1)} %bitcast.5, ...), custom_call_target="tpu_custom_call" | custom-call | tf_op jit(solution)/shard_map/pallas_call | solution.py:704
  81.5 3.6 %shard_map.112 = (bf16[24,9216]{1,0:T(8,128)(2,1)}, bf16[576,512]{1,0:T(8,128)(2,1)}, bf16[16,576]{1,0:T(8,128)(2,1)}, bf16[16,576]{1,0:T(8,128)(2,1)}) custom-call(bf16[24,9216]{1,0:T(8,128)(2,1)} %get-tuple-element.12.refs_0_, bf16[576,512]{1,0:T(8,128)(2,1)} %get-tuple-element.13.refs_1_, bf16[16,576]{1,0:T(8,128)(2,1)} %get-tuple-element.14.refs_2_, ...), custom_call_target="tpu_custom_call" | custom-call | tf_op jit(solution)/shard_map/pallas_call | solution.py:778
